TPU v7x, 512 devices: a whole 4x8x8 slice. The times are simulated.
512 devices in a mesh: dp: 4 (over x), tensor: 128 (over z, y, core).
Axes of the slice: x: 4, y: 8, z: 8, core: 2. Of those that a mesh axis runs over, the one named last changes fastest.
Arguments:
- hidden: bfloat16 [1024, 4096], P(('dp', 'tensor')), parts along dimension 0, may hold values from -16 to 16
- norm_gain: bfloat16 [4096], replicated, may hold values from 0.5 to 1.5
- head_weight: bfloat16 [65536, 4096], P('tensor'), may hold values from -4 to 4
- gate_up: bfloat16 [2, 28672, 1024], P(None, 'tensor', 'dp'), parts along dimension 2, may hold values from -6 to 6
- targets: int32 [1024], P('dp'), parts along dimension 0, may hold values from 0 to 65535
- doc_ids: int32 [1024], P('dp'), parts along dimension 0, may hold values from 0 to 7, never falling along the last dimension, each value on 1 to 64 neighbouring positions
- vocab_codes: int32 [65536], P('tensor'), may hold values from 0 to 127
- hidden_codes: int32 [28672], P('tensor'), may hold values from 0 to 127
- model_codes: int32 [2, 4096], replicated, may hold values from 0 to 127
Outputs:
- resid_grad: bfloat16 [1024, 4096], P(('dp', 'tensor')), parts along dimension 0
- head_features: float32 [32, 4096], P('dp', 'tensor'), parts along dimension 0
- down_features: float32 [32, 4096], P('dp', 'tensor'), parts along dimension 0
There are 4 independent parts, one for each index of `dp`. A program takes and returns all parts, laid end to end along the dimension named above; an argument that names none is the same for every part. Nothing has to cross between parts.
Inputs may be any that keep to these rules, and one draw needn't show every extreme that they name: `doc_ids`: document ids never fall along the tokens; a document has at most 64 tokens.
All inputs are finite; a program needn't handle non-finite values.
Results may differ from a plain program's by a relative error of at most 0.0033.
Values may be sent and summed in bfloat16 or wider, within the bound.
No kernel may reach another device: no remote copies, remote signals or barrier semaphores. Data moves between devices by JAX's collectives and lax.ppermute only.
A program may use at most 64 MiB of HBM per device.

v0:
```python
import jax
import jax.numpy as jnp
from jax import lax
from jax.sharding import PartitionSpec as P

D = 4096
RANK = 64
DOCS = 8


def sign_table(codes):
    slot_ids = jnp.arange(2 * RANK, dtype=jnp.int32)
    matches = (codes[:, None] == slot_ids[None, :]).astype(jnp.float32)
    return matches[:, :RANK] - matches[:, RANK:]


def normalize(rows_in, gain_f32):
    values = rows_in.astype(jnp.float32)
    inv_rms = lax.rsqrt(jnp.mean(values * values, axis=1, keepdims=True) + 1e-05)
    unit_rows = values * inv_rms
    return (inv_rms, unit_rows, (unit_rows * gain_f32).astype(jnp.bfloat16))


def shards(
    hidden,
    norm_gain,
    head_weight,
    gate_up,
    targets,
    doc_ids,
    vocab_codes,
    hidden_codes,
    model_codes,
):
    group_size = lax.axis_size("tensor")
    device_index = lax.axis_index("tensor")
    gain_f32 = norm_gain.astype(jnp.float32)
    vocab_local = head_weight.shape[0]
    inv_rms, unit_rows, own_normed = normalize(hidden, gain_f32)
    normed = lax.all_gather(own_normed, "tensor", axis=0, tiled=True)
    logits = lax.dot_general(
        normed, head_weight, (((1,), (1,)), ((), ())), preferred_element_type=jnp.float32
    )
    local_top = jnp.max(logits, axis=1)
    row_top = lax.pmax(local_top, "tensor")
    shifted = jnp.exp(logits - row_top[:, None])
    denominator = lax.psum(jnp.sum(shifted, axis=1), "tensor")
    vocab_index = device_index * vocab_local + jnp.arange(vocab_local, dtype=jnp.int32)
    onehot = (targets[:, None] == vocab_index[None, :]).astype(jnp.float32)
    dlogits = (shifted / denominator[:, None] - onehot).astype(jnp.bfloat16)
    activation = (
        jax.nn.silu(gate_up[0].astype(jnp.float32)) * gate_up[1].astype(jnp.float32)
    ).astype(jnp.bfloat16)
    vocab_part = jnp.dot(
        dlogits, sign_table(vocab_codes).astype(jnp.bfloat16), preferred_element_type=jnp.float32
    )
    act_part = lax.dot_general(
        activation,
        sign_table(hidden_codes).astype(jnp.bfloat16),
        (((0,), (0,)), ((), ())),
        preferred_element_type=jnp.float32,
    )
    vocab_sketch, act_sketch = lax.psum((vocab_part, act_part), "tensor")
    ff_total = gate_up.shape[1] * group_size
    act_sketch = act_sketch * (RANK / ff_total) ** 0.5
    norm_sketch = (
        jnp.dot(
            normed,
            sign_table(model_codes[0]).astype(jnp.bfloat16),
            preferred_element_type=jnp.float32,
        )
        * (RANK / D) ** 0.5
    )
    grad_table = sign_table(model_codes[1])
    dnormed_rows = lax.psum_scatter(
        jnp.dot(dlogits, head_weight, preferred_element_type=jnp.float32),
        "tensor",
        scatter_dimension=0,
        tiled=True,
    )
    weighted = gain_f32 * dnormed_rows
    inner_mean = jnp.mean(weighted * unit_rows, axis=1, keepdims=True)
    grad_rows = inv_rms * (weighted - unit_rows * inner_mean)
    resid_grad = grad_rows.astype(jnp.bfloat16)
    own_sketch = jnp.dot(grad_rows, grad_table, precision=lax.Precision.HIGHEST)
    grad_sketch = lax.all_gather(own_sketch, "tensor", axis=0, tiled=True)
    grad_sketch = grad_sketch * (RANK / D) ** 0.5
    membership = (doc_ids[None, :] == jnp.arange(DOCS, dtype=jnp.int32)[:, None]).astype(
        jnp.float32
    )
    feature_width = RANK * RANK // group_size

    def doc_features(left_side, right_side):
        spread = membership[:, :, None] * left_side[None, :, :]
        product = jnp.einsum("cti,tj->cij", spread, right_side, precision=lax.Precision.HIGHEST)
        complete = product.reshape(DOCS, RANK * RANK)
        return lax.dynamic_slice_in_dim(complete, device_index * feature_width, feature_width, 1)

    return (
        resid_grad,
        doc_features(vocab_sketch, norm_sketch),
        doc_features(grad_sketch, act_sketch),
    )


def solution(mesh):
    in_specs = (
        P(("dp", "tensor"), None),
        P(),
        P("tensor", None),
        P(None, "tensor", "dp"),
        P("dp"),
        P("dp"),
        P("tensor"),
        P("tensor"),
        P(),
    )
    out_specs = (P(("dp", "tensor"), None), P("dp", "tensor"), P("dp", "tensor"))
    return jax.shard_map(shards, mesh=mesh, in_specs=in_specs, out_specs=out_specs, check_vma=False)
```

profile of v0, /device:TPU:6, one launch (start us, length us, event | category | flops | bytes accessed | tf_op | source)
XLA Modules:
  0.0 875.1 jit_solution(35023871626665761)
XLA Ops:
  7.2 0.0 all-gather.4.cloned.1.call-start
  7.2 0.7 convert_element_type.62
  7.9 0.9 fusion.40
  8.8 1.4 fusion.42
  10.2 0.0 all-gather.4.cloned.1.call-update
  10.2 0.0 all-reduce.4.cloned.1.call-start
  10.3 1.3 dynamic-slice
  12.2 0.7 fusion.43
  12.9 0.8 fusion.27
  13.7 0.8 fusion.18
  14.5 1.8 fusion.28
  16.3 0.9 fusion.48
  17.2 82.0 %all-gather.4.cloned.1.call-done = bf16[128,2,4096]{2,1,0:T(2,128)(2,1)} async-done(((bf16[1,2,4096]{2,1,0:T(2,128)(2,1)}), bf16[128,2,4096]{2,1,0:T(2,128)(2,1)}) %all-gather.4.cloned.1.call-update) | async-done | bytes 2097168 | tf_op jit(solution)/shard_map/all_gather | solution.py:40
  99.2 2.7 reshape.66
  102.0 0.0 copy-start.3
  102.0 3.6 fusion.49
  105.5 249.4 %pmax.7 = f32[256]{0:T(256)S(1)} all-reduce(f32[256]{0:T(256)S(1)} %get-tuple-element.10), channel_id=1, replica_groups=mesh['dp'=4,'tensor'=128] {'tensor'}, use_global_device_ids=true, to_apply=%region_2.0 | all-reduce | flops 256 | bytes 2048 | tf_op jit(solution)/shard_map/pmax | solution.py:45
  354.9 0.2 fusion.12
  355.1 246.8 %psum.21 = f32[256]{0:T(256)S(1)} all-reduce(f32[256]{0:T(256)S(1)} %fusion.12), channel_id=1, replica_groups=mesh['dp'=4,'tensor'=128] {'tensor'}, use_global_device_ids=true, to_apply=%region_4.0 | all-reduce | flops 256 | bytes 2048 | tf_op jit(solution)/shard_map/psum | solution.py:47
  601.9 0.0 copy-done.3
  601.9 5.5 fusion.50
  607.5 1.1 fusion.24
  608.5 0.0 all-reduce.4.cloned.1.call-update
  608.5 3.0 fusion.4
  611.6 0.6 fusion.3
  612.2 0.0 copy-start
  612.2 1.5 fusion.5
  613.7 195.7 %all-reduce.4.cloned.1.call-done = (f32[256,4096]{1,0:T(8,128)}, f32[256,64]{0,1:T(8,128)}, f32[256,64]{0,1:T(8,128)}) async-done(((f32[256,4096]{1,0:T(8,128)}, f32[256,64]{0,1:T(8,128)}, f32[256,64]{0,1:T(8,128)}), (f32[256,4096]{1,0:T(8,128)}, f32[256,64]{0,1:T(8,128)}, f32[256,64]{0,1:T(8,128)})) %all-reduce.4.cloned.1.call-update) | async-done | bytes 4325392
  809.4 0.0 copy-start.2
  809.4 0.0 copy-start.1
  809.4 0.0 copy-done
  809.4 1.2 fusion.37
  810.6 1.6 fusion.46
  812.2 3.7 fusion.6
  815.9 50.2 %all-gather.1 = f32[128,2,64]{2,1,0:T(2,128)S(1)} all-gather(f32[1,2,64]{2,1,0:T(2,128)S(1)} %fusion.6), channel_id=1, replica_groups=mesh['dp'=4,'tensor'=128] {'tensor'}, dimensions={0}, use_global_device_ids=true | all-gather | bytes 66048 | tf_op jit(solution)/shard_map/all_gather | solution.py:86
  866.0 0.1 broadcast_multiply_fusion
  866.1 0.1 copy.13
  866.2 0.0 copy-done.2
  866.2 0.6 fusion.8
  866.8 0.1 reshape.62
  866.9 0.0 copy-done.1
  866.9 0.6 fusion.10
  867.5 0.1 reshape.61
  867.6 0.7 constant_dynamic-slice_fusion
  (3 shorter events, 0.0 us)
Async XLA Ops:
  7.2 92.1 %all-gather.4.cloned.1.call-start = ((), (), s32[]{:S(2)}) async-start(), calls=%async_computation | async-start | bytes 2113536 | tf_op jit(solution)/shard_map/all_gather | solution.py:40
  10.2 799.2 %all-reduce.4.cloned.1.call-start = ((), (), s32[]{:S(2)}) async-start(), calls=%async_computation.1 | async-start | bytes 8650752
  102.0 500.0 %copy-start.3 = (s32[256]{0:T(256)S(1)}, s32[256]{0:T(256)}, u32[]{:S(2)}) copy-start(s32[256]{0:T(256)} %param.13) | copy-start | bytes 3076
  612.2 197.2 %copy-start = (bf16[2,4096]{1,0:T(2,128)(2,1)S(1)}, bf16[2,4096]{1,0:T(2,128)(2,1)}, u32[]{:S(2)}) copy-start(bf16[2,4096]{1,0:T(2,128)(2,1)} %param.9) | copy-start | bytes 49156
  809.4 56.8 %copy-start.2 = (f32[256,64]{0,1:T(8,128)S(1)}, f32[256,64]{0,1:T(8,128)}, u32[]{:S(2)}) copy-start(f32[256,64]{0,1:T(8,128)} %get-tuple-element.5) | copy-start | bytes 196612
  809.4 57.5 %copy-start.1 = (f32[256,64]{0,1:T(8,128)S(1)}, f32[256,64]{0,1:T(8,128)}, u32[]{:S(2)}) copy-start(f32[256,64]{0,1:T(8,128)} %get-tuple-element.4) | copy-start | bytes 196612
Sparse Core Ops, SparseCore 0:
  11.7 87.4 all-gather.3
  608.7 200.6 all-reduce.3
where the time goes:
time: 877 us; the launch traced here: 875 us
  blocking collectives  546 us (62%)
  waiting for transfers between devices  278 us (32%)
  matrix products  18.3 us (2%)
  between operations  14.8 us (2%)
  other arithmetic  11.9 us (1%)
    pmax x1, blocking collectives, shards(): row_top = lax.pmax(local_top, 'tensor')  249 us
    psum x1, blocking collectives, shards(): denominator = lax.psum(jnp.sum(shifted, axis=1), 'tensor')  247 us
    unnamed x3, waiting for transfers between devices  196 us
    all_gather x1, waiting for transfers between devices, shards(): normed = lax.all_gather(own_normed, 'tensor', axis=0, tiled=True)  82 us
    all_gather x1, blocking collectives, shards(): grad_sketch = lax.all_gather(own_sketch, 'tensor', axis=0, tiled=True)  50.2 us
  transfers between devices with their start and end apart: 2, of which 2 were waited for; matrix products, arithmetic and copies ran while one was open for 1% of the time, Pallas kernels for 0%

commit v1 on v0

v1 whole, which is shorter than its diff:
```python
import jax
import jax.numpy as jnp
from jax import lax
from jax.experimental import pallas as pl
from jax.experimental.pallas import tpu as pltpu
from jax.sharding import PartitionSpec as P

D = 4096
RANK = 64
DOCS = 8
PEERS = 64
TOK = 128
LANES = 128
PIECES = D // LANES
VOC = 512
FF = 28672
MIB = 1 << 20

f32 = jnp.float32
bf16 = jnp.bfloat16

NN = (((1,), (0,)), ((), ()))
NT = (((1,), (1,)), ((), ()))
TN = (((0,), (0,)), ((), ()))


def dot(a, b, dims, precision=None):
    return lax.dot_general(a, b, dims, precision=precision, preferred_element_type=f32)


def sign_rows(codes_row):
    slots = lax.broadcasted_iota(jnp.int32, (RANK, codes_row.shape[1]), 0)
    plus = (codes_row == slots).astype(f32)
    minus = (codes_row == slots + RANK).astype(f32)
    return (plus - minus).astype(bf16)


def token_piece(ref, piece):
    first = ref[pl.ds(piece, PEERS, stride=2 * PIECES), :]
    second = ref[pl.ds(PIECES + piece, PEERS, stride=2 * PIECES), :]
    return jnp.concatenate([first, second], axis=0)


def call(kernel, outs, scratch, n_in, flops, bytes_accessed, any_inputs=(), vmem=48 * MIB):
    specs = [
        pl.BlockSpec(memory_space=pl.ANY if i in any_inputs else pltpu.VMEM) for i in range(n_in)
    ]
    return pl.pallas_call(
        kernel,
        out_shape=outs,
        in_specs=specs,
        out_specs=jax.tree.map(lambda _: pl.BlockSpec(memory_space=pltpu.VMEM), outs),
        scratch_shapes=scratch,
        compiler_params=pltpu.CompilerParams(vmem_limit_bytes=vmem),
        cost_estimate=pl.CostEstimate(
            flops=flops, bytes_accessed=bytes_accessed, transcendentals=0
        ),
    )


def act_kernel(gate_up, codes, out):
    gate = gate_up[0].astype(f32)
    act = (gate / (1.0 + jnp.exp(-gate)) * gate_up[1].astype(f32)).astype(bf16)
    out[...] = dot(sign_rows(codes[...]), act, NN)


def table_kernel(codes, out):
    for block in range(8):
        cols = pl.ds(block * 512, 512)
        out[0:RANK, cols] = sign_rows(codes[0:1, cols])
        out[RANK : 2 * RANK, cols] = sign_rows(codes[1:2, cols])


def norm_pieces(x, gain, xf, hid, normed):
    xf[...] = x[...].astype(f32)
    squares = jnp.zeros((TOK, LANES), f32)
    for k in range(PIECES):
        piece = token_piece(xf, k)
        squares = squares + piece * piece
        hid[:, k * LANES : (k + 1) * LANES] = piece.astype(bf16)
    inv = lax.rsqrt(jnp.sum(squares, axis=1, keepdims=True) * (1.0 / D) + 1e-05)
    for k in range(PIECES):
        cols = slice(k * LANES, (k + 1) * LANES)
        unit = hid[:, cols].astype(f32) * inv
        normed[:, cols] = (unit * gain[k : k + 1, :]).astype(bf16)
    return squares


def score_kernel(x, gain, w_own, w_par, act, logits, payload, xf, hid, normed, w, sems):
    copies = []
    for block in range(4):
        source = w_own if block < 2 else w_par
        copy = pltpu.make_async_copy(
            source.at[pl.ds((block % 2) * 256, 256)], w.at[pl.ds(block * 256, 256)], sems.at[block]
        )
        copy.start()
        copies.append(copy)
    norm_pieces(x, gain, xf, hid, normed)
    for block in range(4):
        copies[block].wait()
        rows = pl.ds(block * 256, 256)
        logits[rows, :] = dot(w[rows, :], normed[...], NT)
    scores = logits[...]
    top = jnp.max(scores, axis=0, keepdims=True)
    total = jnp.sum(jnp.exp(scores - top), axis=0, keepdims=True)
    payload[pl.ds(0, PEERS, stride=4), :] = jnp.broadcast_to(top, (PEERS, LANES))
    payload[pl.ds(1, PEERS, stride=4), :] = jnp.broadcast_to(total, (PEERS, LANES))
    payload[pl.ds(2, PEERS, stride=4), :] = jnp.broadcast_to(act[...], (PEERS, LANES))
    payload[pl.ds(3, PEERS, stride=4), :] = jnp.zeros((PEERS, LANES), f32)


def norm_sketch_kernel(x, gain, table, aux, xf, hid, normed):
    squares = norm_pieces(x, gain, xf, hid, normed)
    sums = jnp.sum(squares.T, axis=0, keepdims=True)
    inv = lax.rsqrt(sums * (1.0 / D) + 1e-05)
    aux[0:RANK, :] = dot(table[0:RANK, :], normed[...], NT) * (RANK / D) ** 0.5
    aux[RANK : 2 * RANK, :] = dot(table[RANK : 2 * RANK, :], hid[...], NT) * inv
    aux[2 * RANK : 2 * RANK + 8, :] = jnp.broadcast_to(inv, (8, LANES))


def grad_kernel(stats, logits, hit, w_own, w_par, blocks, dl_out, mean_out, dn_out, df, w, sems):
    copies = []
    for chunk in range(8):
        cols = pl.ds(chunk * 512, 512)
        for half, source in enumerate((w_own, w_par)):
            copy = pltpu.make_async_copy(
                source.at[:, cols], w.at[pl.ds(half * VOC, VOC), cols], sems.at[chunk, half]
            )
            copy.start()
            copies.append(copy)
    tops = stats[pl.ds(0, PEERS, stride=4), :]
    totals = stats[pl.ds(1, PEERS, stride=4), :]
    top = jnp.max(tops, axis=0, keepdims=True)
    denominator = jnp.sum(totals * jnp.exp(tops - top), axis=0, keepdims=True)
    scores = logits[...]
    rows = lax.broadcasted_iota(jnp.int32, (2 * VOC, LANES), 0)
    onehot = (rows == hit[0:1, :]).astype(f32)
    dl32 = jnp.exp(scores - top) / denominator - onehot
    dl = dl32.astype(bf16)
    dl_out[...] = dl
    mean = jnp.sum(dl.astype(f32) * scores, axis=0, keepdims=True) * (1.0 / D)
    mean_out[...] = jnp.broadcast_to(mean, (8, LANES))
    dl_t = dl32.T.astype(bf16)
    for chunk in range(8):
        copies[2 * chunk].wait()
        copies[2 * chunk + 1].wait()
        cols = slice(chunk * 512, (chunk + 1) * 512)
        dn = dot(dl_t, w[:, cols], NN)
        dn_out[:, cols] = dn
        for k in range(4):
            piece = chunk * 4 + k
            lanes = slice(k * LANES, (k + 1) * LANES)
            df[pl.ds(piece, PEERS, stride=2 * PIECES), :] = dn[0:PEERS, lanes]
            df[pl.ds(PIECES + piece, PEERS, stride=2 * PIECES), :] = dn[PEERS:TOK, lanes]
    blocks[...] = df[...].astype(bf16)


def sketch_kernel(dl, mean, dn, codes, table, gain, aux, columns):
    vocab_sketch = dot(sign_rows(codes[...]), dl[...], NN)
    weighted = dn[...] * gain[...]
    high = weighted.astype(bf16)
    low = (weighted - high.astype(f32)).astype(bf16)
    signs = table[RANK : 2 * RANK, :]
    sketch = dot(signs, high, NT) + dot(signs, low, NT)
    unit_sketch = aux[RANK : 2 * RANK, :]
    inv = aux[2 * RANK : 2 * RANK + 1, :]
    grad_sketch = inv * (sketch - unit_sketch * mean[0:1, :]) * (RANK / D) ** 0.5
    columns[pl.ds(0, PEERS, stride=2), :] = vocab_sketch
    columns[pl.ds(1, PEERS, stride=2), :] = grad_sketch


def feature_kernel(columns, stats, aux, docs, out):
    vocab_column = jnp.sum(columns[pl.ds(0, PEERS, stride=2), :], axis=0, keepdims=True)
    grad_column = jnp.sum(columns[pl.ds(1, PEERS, stride=2), :], axis=0, keepdims=True)
    acts = stats[pl.ds(2, PEERS, stride=4), :]
    act_sketch = jnp.concatenate([acts[:, 0:RANK], acts[:, RANK : 2 * RANK]], axis=0)
    act_sketch = act_sketch * (RANK / FF) ** 0.5
    ids = lax.broadcasted_iota(jnp.int32, (DOCS, LANES), 0)
    member = (docs[0:1, :] == ids).astype(f32)
    high = lax.Precision.HIGHEST
    out[0:DOCS, :] = dot(member * vocab_column, aux[0:RANK, :], NT, high)
    out[DOCS : 2 * DOCS, :] = dot(member * grad_column, act_sketch, NN, high)


def resid_kernel(blocks, hidden, gain, out):
    total = jnp.zeros((2 * PIECES, LANES), f32)
    for source in range(PEERS):
        total = total + blocks[source * 2 * PIECES : (source + 1) * 2 * PIECES, :].astype(f32)
    for token in range(2):
        rows = slice(token * PIECES, (token + 1) * PIECES)
        values = hidden[rows, :].astype(f32)
        inv = lax.rsqrt(jnp.sum(values * values, keepdims=True) * (1.0 / D) + 1e-05)
        unit = values * inv
        weighted = gain[...] * total[rows, :]
        inner = jnp.sum(weighted * unit, keepdims=True) * (1.0 / D)
        out[rows, :] = (inv * (weighted - unit * inner)).astype(bf16)


def shards(
    hidden,
    norm_gain,
    head_weight,
    gate_up,
    targets,
    doc_ids,
    vocab_codes,
    hidden_codes,
    model_codes,
):
    index = lax.axis_index("tensor")
    core = lax.rem(index, 2)
    groups = [list(range(0, 2 * PEERS, 2)), list(range(1, 2 * PEERS, 2))]
    partner = [(i, i ^ 1) for i in range(2 * PEERS)]
    gain32 = norm_gain.astype(f32)
    gain_row = gain32.reshape(1, D)
    gain_blk = gain32.reshape(PIECES, LANES)
    own_rows = hidden.reshape(2 * PIECES, LANES)

    def exchange(rows):
        return lax.all_to_all(rows, "tensor", 0, 0, axis_index_groups=groups, tiled=True)

    with jax.named_scope("gather_hidden"):
        spread = jnp.broadcast_to(own_rows[None], (PEERS, 2 * PIECES, LANES))
        gathered = exchange(spread).reshape(PEERS * 2 * PIECES, LANES)
    with jax.named_scope("partner_rows"):
        w_par = lax.ppermute(head_weight, "tensor", partner)
        codes_par = lax.ppermute(vocab_codes, "tensor", partner)
        codes = jnp.concatenate([vocab_codes, codes_par]).reshape(1, 2 * VOC)
    with jax.named_scope("activations"):
        act_part = call(act_kernel, jax.ShapeDtypeStruct((RANK, 256), f32), [], 2, 8000000, 300000)(
            gate_up, hidden_codes.reshape(1, -1)
        )
        act_blocks = act_part.T.reshape(2 * PEERS, 1, LANES)
        act_all = lax.all_to_all(act_blocks, "tensor", 0, 0, tiled=True)
        act_own = jnp.sum(act_all, axis=0)
    with jax.named_scope("tables"):
        table = call(
            table_kernel, jax.ShapeDtypeStruct((2 * RANK, D), bf16), [], 1, 4000000, 1100000
        )(model_codes)
        ids = jnp.stack([targets, doc_ids]).reshape(2, PEERS, 2, 2)
        ids = lax.dynamic_index_in_dim(ids, core, axis=2, keepdims=False)
        ids = ids.transpose(0, 2, 1).reshape(2, TOK)
        relative = ids[0] - index * VOC
        relative_par = ids[0] - (index + 1 - 2 * core) * VOC
        hit = jnp.where(
            (relative >= 0) & (relative < VOC),
            relative,
            jnp.where((relative_par >= 0) & (relative_par < VOC), relative_par + VOC, -1),
        ).reshape(1, TOK)
        docs = ids[1].reshape(1, TOK)

    norm_scratch = [
        pltpu.VMEM((PEERS * 2 * PIECES, LANES), f32),
        pltpu.VMEM((TOK, D), bf16),
        pltpu.VMEM((TOK, D), bf16),
    ]
    with jax.named_scope("scores"):
        logits, payload = call(
            score_kernel,
            (
                jax.ShapeDtypeStruct((2 * VOC, TOK), f32),
                jax.ShapeDtypeStruct((PEERS * 4, LANES), f32),
            ),
            norm_scratch + [pltpu.VMEM((2 * VOC, D), bf16), pltpu.SemaphoreType.DMA((4,))],
            5,
            1 << 30,
            10 * MIB,
            any_inputs=(2, 3),
        )(gathered, gain_blk, head_weight, w_par, act_own)
    with jax.named_scope("statistics"):
        stats = exchange(payload.reshape(PEERS, 4, LANES)).reshape(PEERS * 4, LANES)
    with jax.named_scope("norm_sketch"):
        aux = call(
            norm_sketch_kernel,
            jax.ShapeDtypeStruct((2 * RANK + 8, LANES), f32),
            norm_scratch,
            3,
            200000000,
            3 * MIB,
        )(gathered, gain_blk, table)
    with jax.named_scope("dnormed"):
        blocks, dl, mean, dn = call(
            grad_kernel,
            (
                jax.ShapeDtypeStruct((PEERS * 2 * PIECES, LANES), bf16),
                jax.ShapeDtypeStruct((2 * VOC, TOK), bf16),
                jax.ShapeDtypeStruct((8, LANES), f32),
                jax.ShapeDtypeStruct((TOK, D), f32),
            ),
            [
                pltpu.VMEM((PEERS * 2 * PIECES, LANES), f32),
                pltpu.VMEM((2 * VOC, D), bf16),
                pltpu.SemaphoreType.DMA((8, 2)),
            ],
            5,
            1 << 30,
            12 * MIB,
            any_inputs=(3, 4),
        )(stats, logits, hit, head_weight, w_par)
    with jax.named_scope("scatter_dnormed"):
        received = exchange(blocks.reshape(PEERS, 2 * PIECES, LANES))
        received = received.reshape(PEERS * 2 * PIECES, LANES)
    with jax.named_scope("sketches"):
        columns = call(
            sketch_kernel,
            jax.ShapeDtypeStruct((2 * PEERS, LANES), f32),
            [],
            7,
            200000000,
            4 * MIB,
        )(dl, mean, dn, codes, table, gain_row, aux)
        columns = exchange(columns.reshape(PEERS, 2, LANES)).reshape(2 * PEERS, LANES)
    with jax.named_scope("features"):
        features = call(
            feature_kernel,
            jax.ShapeDtypeStruct((2 * DOCS, RANK), f32),
            [],
            4,
            2000000,
            300000,
        )(columns, stats, aux, docs)
        half = RANK // 2
        mine = lax.dynamic_slice_in_dim(features, core * half, half, 1)
        other = lax.dynamic_slice_in_dim(features, (1 - core) * half, half, 1)
        features = mine + lax.ppermute(other, "tensor", partner)
    with jax.named_scope("resid_grad"):
        resid = call(
            resid_kernel,
            jax.ShapeDtypeStruct((2 * PIECES, LANES), bf16),
            [],
            3,
            2000000,
            MIB,
        )(received, own_rows, gain_blk)
        resid = resid.reshape(2, D)
    return resid, features[:DOCS], features[DOCS:]


def solution(mesh):
    in_specs = (
        P(("dp", "tensor"), None),
        P(),
        P("tensor", None),
        P(None, "tensor", "dp"),
        P("dp"),
        P("dp"),
        P("tensor"),
        P("tensor"),
        P(),
    )
    out_specs = (P(("dp", "tensor"), None), P("dp", "tensor"), P("dp", "tensor"))
    return jax.shard_map(shards, mesh=mesh, in_specs=in_specs, out_specs=out_specs, check_vma=False)
```

time: 877 us -> 156 us (0.18)
  blocking collectives: 546 us -> 16 us
  waiting for transfers between devices: 278 us -> 69.6 us
  starting transfers between devices: 0.08 us -> 39.9 us
  Pallas kernels: 0 us -> 18.6 us
  matrix products: 18.3 us -> 0 us
  between operations: 14.8 us -> 0.83 us
  other arithmetic: 11.9 us -> 0.26 us
    pmax x1 -> x0, blocking collectives: 249 us -> none  [shards(): row_top = lax.pmax(local_top, 'tensor')]
    psum x1 -> x0, blocking collectives: 247 us -> none  [shards(): denominator = lax.psum(jnp.sum(shifted, axis=1), 'tensor')]
    unnamed x3 -> x0, waiting for transfers between devices: 196 us -> none
    all_gather x1 -> x0, waiting for transfers between devices: 82 us -> none  [shards(): normed = lax.all_gather(own_normed, 'tensor', axis=0, tiled=True)]
    all_to_all x0 -> x4, waiting for transfers between devices: none -> 68.5 us  [the longest x3 58.1 us: exchange(): lax.all_to_all(rows, 'tensor', 0, 0, axis_index_groups=groups, tiled=True)]
    all_gather x1 -> x0, blocking collectives: 50.2 us -> none  [shards(): grad_sketch = lax.all_gather(own_sketch, 'tensor', axis=0, tiled=True)]
    all_to_all x0 -> x4, starting transfers between devices: none -> 34.2 us  [the longest x1 17.9 us: shards(): act_all = lax.all_to_all(act_blocks, 'tensor', 0, 0, tiled=True)]
    pallas_call x0 -> x8, Pallas kernels: none -> 18.6 us  [the longest x1 7.9 us: shards(): call(score_kernel, (jax.ShapeDtypeStruct((2 * VOC, TOK), f32), jax.ShapeD...]
  transfers between devices with their start and end apart: 2 -> 7, of which waited for: 2 -> 5; matrix products, arithmetic and copies ran while one was open for 1% -> 4% of each run, Pallas kernels for 0% -> 7%
where the time goes in v1:
time: 156 us; the launch traced here: 155 us
  waiting for transfers between devices  69.6 us (45%)
  starting transfers between devices  39.9 us (26%)
  Pallas kernels  18.6 us (12%)
  blocking collectives  16 us (10%)
  local copies, waits for them, and re-layouts  9.98 us (6%)
    all_to_all x3, waiting for transfers between devices, exchange(): lax.all_to_all(rows, 'tensor', 0, 0, axis_index_groups=groups, tiled=True)  58.1 us
    all_to_all x1, starting transfers between devices, shards(): act_all = lax.all_to_all(act_blocks, 'tensor', 0, 0, tiled=True)  17.9 us
    all_to_all x3, starting transfers between devices, exchange(): lax.all_to_all(rows, 'tensor', 0, 0, axis_index_groups=groups, tiled=True)  16.3 us
    all_to_all x1, blocking collectives, exchange(): lax.all_to_all(rows, 'tensor', 0, 0, axis_index_groups=groups, tiled=True)  16 us
    all_to_all x1, waiting for transfers between devices, shards(): act_all = lax.all_to_all(act_blocks, 'tensor', 0, 0, tiled=True)  10.4 us
    pallas_call x1, Pallas kernels, shards(): call(score_kernel, (jax.ShapeDtypeStruct((2 * VOC, TOK), f32), jax.ShapeD...  7.9 us
    pallas_call x1, Pallas kernels, shards(): call(grad_kernel, (jax.ShapeDtypeStruct((PEERS * 2 * PIECES, LANES), bf16...  6.25 us
    unnamed x12, local copies, waits for them, and re-layouts  3.81 us
  transfers between devices with their start and end apart: 7, of which 5 were waited for; matrix products, arithmetic and copies ran while one was open for 4% of the time, Pallas kernels for 7%

profile of v1, /device:TPU:6, one launch (start us, length us, event | category | flops | bytes accessed | tf_op | source)
XLA Modules:
  0.0 155.2 jit_solution(3115582555522232715)
XLA Ops:
  0.6 1.9 %collective-permute-start = (bf16[512,4096]{1,0:T(8,128)(2,1)}, bf16[512,4096]{1,0:T(8,128)(2,1)}, u32[]{:S(2)}, u32[]{:S(2)}) collective-permute-start(bf16[512,4096]{1,0:T(8,128)(2,1)} %w_own.3), channel_id=1, source_target_pairs={{0,1},{1,0},{2,3},{3,2},{4,5},{5,4},{6,7},{7,6},{8,9},{9,8},{10,11... | collective-permute-start | bytes 12582920 | tf_op jit(solution)/shard_map/partner_rows/ppermute | solution.py:226
  2.6 0.0 copy-start.1
  2.6 0.9 copy-done.1
  3.5 0.0 copy-start.3
  3.5 0.7 copy-done.3
  4.2 0.0 copy-start.4
  4.2 0.2 activations.1
  4.4 0.1 copy.15
  4.5 0.7 reshape.120
  5.2 17.9 %all-to-all-start.1 = ((f32[128,1,128]{2,1,0:T(1,128)}), f32[128,1,128]{2,1,0:T(1,128)S(1)}, u32[]{:S(2)}, u32[]{:S(2)}) async-start(f32[128,1,128]{2,1,0:T(1,128)} %bitcast.4), calls=%async_computation.1 | async-start | bytes 131072 | tf_op jit(solution)/shard_map/activations/all_to_all | solution.py:234
  23.1 0.7 broadcast_in_dim.11.hidden
  23.9 10.4 %all-to-all-done.1 = f32[128,1,128]{2,1,0:T(1,128)S(1)} async-done(((f32[128,1,128]{2,1,0:T(1,128)}), f32[128,1,128]{2,1,0:T(1,128)S(1)}, u32[]{:S(2)}, u32[]{:S(2)}) %all-to-all-start.1) | async-done | bytes 65568 | tf_op jit(solution)/shard_map/activations/all_to_all | solution.py:234
  34.2 1.2 broadcast_in_dim.12
  35.5 4.7 %all-to-all-start = ((bf16[64,64,128]{2,1,0:T(8,128)(2,1)}), bf16[64,64,128]{2,1,0:T(8,128)(2,1)S(1)}, u32[]{:S(2)}, u32[]{:S(2)}) async-start(bf16[64,64,128]{2,1,0:T(8,128)(2,1)} %broadcast_in_dim.12), calls=%async_computation | async-start | bytes 2097152 | tf_op jit(solution)/shard_map/gather_hidden/all_to_all | solution.py:220
  40.1 1.9 %collective-permute-start.1 = (s32[512]{0:T(512)}, s32[512]{0:T(512)S(1)}, u32[]{:S(2)}, u32[]{:S(2)}) collective-permute-start(s32[512]{0:T(512)} %param.15), channel_id=1, source_target_pairs={{0,1},{1,0},{2,3},{3,2},{4,5},{5,4},{6,7},{7,6},{8,9},{9,8},{10,11... | collective-permute-start | bytes 6152 | tf_op jit(solution)/shard_map/partner_rows/ppermute | solution.py:227
  42.1 0.8 stack.9
  42.9 0.1 copy.17
  43.0 0.8 stack.10
  43.8 0.1 copy.18
  44.0 0.1 select_n.37
  44.0 0.1 sub.38
  44.1 0.0 copy-done.4
  44.1 0.2 reduce_sum.11
  44.3 25.8 %all-to-all-done = bf16[64,64,128]{2,1,0:T(8,128)(2,1)S(1)} async-done(((bf16[64,64,128]{2,1,0:T(8,128)(2,1)}), bf16[64,64,128]{2,1,0:T(8,128)(2,1)S(1)}, u32[]{:S(2)}, u32[]{:S(2)}) %all-to-all-start) | async-done | bytes 1048608 | tf_op jit(solution)/shard_map/gather_hidden/all_to_all | solution.py:220
  70.1 0.0 collective-permute-done.w_par
  70.1 2.2 %copy-done = bf16[512,4096]{1,0:T(8,128)(2,1)S(1)} copy-done((bf16[512,4096]{1,0:T(8,128)(2,1)S(1)}, bf16[512,4096]{1,0:T(8,128)(2,1)}, u32[]{:S(2)}) %copy-start) | copy-done | bytes 4194328
  72.3 7.9 %scores.1 = (f32[1024,128]{1,0:T(8,128)S(1)}, f32[256,128]{1,0:T(8,128)}) custom-call(bf16[4096,128]{1,0:T(8,128)(2,1)S(1)} %bitcast.19, f32[32,128]{1,0:T(8,128)S(1)} %get-tuple-element.18.gain, bf16[512,4096]{1,0:T(8,128)(2,1)S(1)} %copy-done, bf16[512,4096]{1,0:T(8,128)(2,1)} %collective-permute-done.w_par, f32[1,128]{1,0:T(1,128)S(1)} %bitcast.29), custom_call_target="tpu_custom_call" | custom-call | flops 1073741824 | bytes 10485760 | tf_op jit(solution)/shard_map/scores/pallas_call | solution.py:258
  80.2 7.0 %all-to-all-start.2 = ((f32[64,4,128]{2,1,0:T(4,128)}), f32[64,4,128]{2,1,0:T(4,128)S(1)}, u32[]{:S(2)}, u32[]{:S(2)}) async-start(f32[64,4,128]{2,1,0:T(4,128)} %bitcast.6), calls=%async_computation.2 | async-start | bytes 262144 | tf_op jit(solution)/shard_map/statistics/all_to_all | solution.py:220
  87.2 0.0 copy-done.2
  87.2 0.4 tables.1.table
  87.6 0.0 collective-permute-done.1
  87.6 0.0 copy-done.5
  87.6 2.3 %norm_sketch.1.aux = f32[136,128]{1,0:T(8,128)S(1)} custom-call(bf16[4096,128]{1,0:T(8,128)(2,1)S(1)} %bitcast.20, f32[32,128]{1,0:T(8,128)S(1)} %get-tuple-element.18.gain, bf16[128,4096]{1,0:T(8,128)(2,1)S(1)} %tables.1.table), custom_call_target="tpu_custom_call" | custom-call | flops 200000000 | bytes 3145728 | tf_op jit(solution)/shard_map/norm_sketch/pallas_call | solution.py:273
  89.9 9.9 %all-to-all-done.2 = f32[64,4,128]{2,1,0:T(4,128)S(1)} async-done(((f32[64,4,128]{2,1,0:T(4,128)}), f32[64,4,128]{2,1,0:T(4,128)S(1)}, u32[]{:S(2)}, u32[]{:S(2)}) %all-to-all-start.2) | async-done | bytes 131104 | tf_op jit(solution)/shard_map/statistics/all_to_all | solution.py:220
  99.7 6.3 %dnormed.1 = (bf16[4096,128]{1,0:T(8,128)(2,1)}, bf16[1024,128]{1,0:T(8,128)(2,1)S(1)}, f32[8,128]{1,0:T(8,128)S(1)}, f32[128,4096]{1,0:T(8,128)S(1)}) custom-call(f32[256,128]{1,0:T(8,128)S(1)} %bitcast.22, f32[1024,128]{1,0:T(8,128)S(1)} %get-tuple-element.10.logits, s32[1,128]{1,0:T(1,128)S(1)} %and_select_fusion.1.hit, bf16[512,4096]{1,0:T(8,128)(2,1)} %w_own.3, ...), custom_call_target="tpu_custom_call" | custom-call | flops 1073741824 | bytes 12582912 | tf_op jit(solution)/shard_map/dnormed/pallas_call | solution.py:282
  106.0 0.9 sketches.1
  106.9 16.0 %all_to_all.25 = f32[64,2,128]{2,1,0:T(2,128)S(1)} all-to-all(f32[64,2,128]{2,1,0:T(2,128)S(1)} %bitcast.24), channel_id=1, replica_groups={{0,2,4,6,8,10,12,14,16,18,20,22,24,26,28,30,32,34,36,38,40,42,44,46,48,..., dimensions={0} | all-to-all | bytes 131072 | tf_op jit(solution)/shard_map/sketches/all_to_all | solution.py:220
  122.9 4.7 %all-to-all-start.3 = ((bf16[64,64,128]{2,1,0:T(8,128)(2,1)}), bf16[64,64,128]{2,1,0:T(8,128)(2,1)S(1)}, u32[]{:S(2)}, u32[]{:S(2)}) async-start(bf16[64,64,128]{2,1,0:T(8,128)(2,1)} %bitcast.10), calls=%async_computation.3 | async-start | bytes 2097152 | tf_op jit(solution)/shard_map/scatter_dnormed/all_to_all | solution.py:220
  127.6 0.1 slice.19.docs
  127.7 0.3 features.1
  127.9 0.1 constant_dynamic-slice_fusion
  128.0 1.9 %collective-permute-start.2 = (f32[16,32]{1,0:T(8,128)S(1)}, f32[16,32]{1,0:T(8,128)S(1)}, u32[]{:S(2)}, u32[]{:S(2)}) collective-permute-start(f32[16,32]{1,0:T(8,128)S(1)} %constant_dynamic-slice_fusion), channel_id=1, source_target_pairs={{0,1},{1,0},{2,3},{3,2},{4,5},{5,4},{6,7},{7,6},{8,9},{9,8},{10,11... | collective-permute-start | bytes 6152 | tf_op jit(solution)/shard_map/features/ppermute | solution.py:325
  130.0 1.1 collective-permute-done.2
  131.1 0.1 dynamic-slice_add_fusion
  131.2 0.6 fusion.2
  131.8 22.4 %all-to-all-done.3 = bf16[64,64,128]{2,1,0:T(8,128)(2,1)S(1)} async-done(((bf16[64,64,128]{2,1,0:T(8,128)(2,1)}), bf16[64,64,128]{2,1,0:T(8,128)(2,1)S(1)}, u32[]{:S(2)}, u32[]{:S(2)}) %all-to-all-start.3) | async-done | bytes 1048608 | tf_op jit(solution)/shard_map/scatter_dnormed/all_to_all | solution.py:220
  154.2 0.4 resid_grad.1
  154.6 0.6 reshape.125
  (8 shorter events, 0.0 us)
Async XLA Ops:
  0.6 69.4 %collective-permute-start = (bf16[512,4096]{1,0:T(8,128)(2,1)}, bf16[512,4096]{1,0:T(8,128)(2,1)}, u32[]{:S(2)}, u32[]{:S(2)}) collective-permute-start(bf16[512,4096]{1,0:T(8,128)(2,1)} %w_own.3), channel_id=1, source_target_pairs={{0,1},{1,0},{2,3},{3,2},{4,5},{5,4},{6,7},{7,6},{8,9},{9,8},{10,11... | collective-permute-start | bytes 12582920 | tf_op jit(solution)/shard_map/partner_rows/ppermute | solution.py:226
  2.6 0.9 copy-start.1
  3.5 0.7 copy-start.3
  4.2 39.9 %copy-start.4 = (bf16[4096]{0:T(1024)(128)(2,1)S(1)}, bf16[4096]{0:T(1024)(128)(2,1)}, u32[]{:S(2)}) copy-start(bf16[4096]{0:T(1024)(128)(2,1)} %param.10) | copy-start | bytes 24580
  5.2 29.0 %all-to-all-start.1 = ((f32[128,1,128]{2,1,0:T(1,128)}), f32[128,1,128]{2,1,0:T(1,128)S(1)}, u32[]{:S(2)}, u32[]{:S(2)}) async-start(f32[128,1,128]{2,1,0:T(1,128)} %bitcast.4), calls=%async_computation.1 | async-start | bytes 131072 | tf_op jit(solution)/shard_map/activations/all_to_all | solution.py:234
  35.5 34.6 %all-to-all-start = ((bf16[64,64,128]{2,1,0:T(8,128)(2,1)}), bf16[64,64,128]{2,1,0:T(8,128)(2,1)S(1)}, u32[]{:S(2)}, u32[]{:S(2)}) async-start(bf16[64,64,128]{2,1,0:T(8,128)(2,1)} %broadcast_in_dim.12), calls=%async_computation | async-start | bytes 2097152 | tf_op jit(solution)/shard_map/gather_hidden/all_to_all | solution.py:220
  40.1 47.4 %collective-permute-start.1 = (s32[512]{0:T(512)}, s32[512]{0:T(512)S(1)}, u32[]{:S(2)}, u32[]{:S(2)}) collective-permute-start(s32[512]{0:T(512)} %param.15), channel_id=1, source_target_pairs={{0,1},{1,0},{2,3},{3,2},{4,5},{5,4},{6,7},{7,6},{8,9},{9,8},{10,11... | collective-permute-start | bytes 6152 | tf_op jit(solution)/shard_map/partner_rows/ppermute | solution.py:227
  70.1 2.2 %copy-start = (bf16[512,4096]{1,0:T(8,128)(2,1)S(1)}, bf16[512,4096]{1,0:T(8,128)(2,1)}, u32[]{:S(2)}) copy-start(bf16[512,4096]{1,0:T(8,128)(2,1)} %w_own.3) | copy-start | bytes 12582916
  72.3 14.9 %copy-start.2 = (s32[2,4096]{1,0:T(2,128)S(1)}, s32[2,4096]{1,0:T(2,128)}, u32[]{:S(2)}) copy-start(s32[2,4096]{1,0:T(2,128)} %codes.1) | copy-start | bytes 98308
  72.3 15.3 %copy-start.5 = (s32[512]{0:T(512)S(1)}, s32[512]{0:T(512)}, u32[]{:S(2)}) copy-start(s32[512]{0:T(512)} %param.15) | copy-start | bytes 6148
  80.2 19.6 %all-to-all-start.2 = ((f32[64,4,128]{2,1,0:T(4,128)}), f32[64,4,128]{2,1,0:T(4,128)S(1)}, u32[]{:S(2)}, u32[]{:S(2)}) async-start(f32[64,4,128]{2,1,0:T(4,128)} %bitcast.6), calls=%async_computation.2 | async-start | bytes 262144 | tf_op jit(solution)/shard_map/statistics/all_to_all | solution.py:220
  122.9 31.3 %all-to-all-start.3 = ((bf16[64,64,128]{2,1,0:T(8,128)(2,1)}), bf16[64,64,128]{2,1,0:T(8,128)(2,1)S(1)}, u32[]{:S(2)}, u32[]{:S(2)}) async-start(bf16[64,64,128]{2,1,0:T(8,128)(2,1)} %bitcast.10), calls=%async_computation.3 | async-start | bytes 2097152 | tf_op jit(solution)/shard_map/scatter_dnormed/all_to_all | solution.py:220
  128.0 3.1 %collective-permute-start.2 = (f32[16,32]{1,0:T(8,128)S(1)}, f32[16,32]{1,0:T(8,128)S(1)}, u32[]{:S(2)}, u32[]{:S(2)}) collective-permute-start(f32[16,32]{1,0:T(8,128)S(1)} %constant_dynamic-slice_fusion), channel_id=1, source_target_pairs={{0,1},{1,0},{2,3},{3,2},{4,5},{5,4},{6,7},{7,6},{8,9},{9,8},{10,11... | collective-permute-start | bytes 6152 | tf_op jit(solution)/shard_map/features/ppermute | solution.py:325

commit v2 on v1

v2 whole, which is shorter than its diff:
```python
import jax
import jax.numpy as jnp
from jax import lax
from jax.experimental import pallas as pl
from jax.experimental.pallas import tpu as pltpu
from jax.sharding import PartitionSpec as P

D = 4096
RANK = 64
DOCS = 8
PEERS = 64
TOK = 128
LANES = 128
PIECES = D // LANES
VOC = 512
FF = 28672
PITCH = 2 * PIECES + 8
CHUNK = 512
MIB = 1 << 20

f32 = jnp.float32
bf16 = jnp.bfloat16

NN = (((1,), (0,)), ((), ()))
NT = (((1,), (1,)), ((), ()))
TN = (((0,), (0,)), ((), ()))


def dot(a, b, dims, precision=None):
    return lax.dot_general(a, b, dims, precision=precision, preferred_element_type=f32)


def sign_rows(codes_row):
    slots = lax.broadcasted_iota(jnp.int32, (RANK, codes_row.shape[1]), 0)
    plus = (codes_row == slots).astype(f32)
    minus = (codes_row == slots + RANK).astype(f32)
    return (plus - minus).astype(bf16)


def token_piece(ref, piece):
    first = ref[pl.ds(piece, PEERS, stride=PITCH), :]
    second = ref[pl.ds(PIECES + piece, PEERS, stride=PITCH), :]
    return jnp.concatenate([first, second], axis=0)


def call(kernel, outs, scratch, n_in, flops, bytes_accessed, any_inputs=(), any_outs=(), vmem=32 * MIB):
    specs = [
        pl.BlockSpec(memory_space=pltpu.HBM if i in any_inputs else pltpu.VMEM) for i in range(n_in)
    ]
    leaves, tree = jax.tree.flatten(outs)
    out_specs = tree.unflatten(
        [
            pl.BlockSpec(memory_space=pltpu.HBM if i in any_outs else pltpu.VMEM)
            for i in range(len(leaves))
        ]
    )
    leaves = [
        pltpu.HBM(leaf.shape, leaf.dtype) if i in any_outs else leaf
        for i, leaf in enumerate(leaves)
    ]
    inner = pl.pallas_call(
        kernel,
        out_shape=tree.unflatten(leaves),
        in_specs=specs,
        out_specs=out_specs,
        scratch_shapes=scratch,
        compiler_params=pltpu.CompilerParams(vmem_limit_bytes=vmem),
        cost_estimate=pl.CostEstimate(
            flops=flops, bytes_accessed=bytes_accessed, transcendentals=0
        ),
    )

    def run(*args):
        return inner(
            *[
                pltpu.with_memory_space_constraint(arg, pltpu.HBM) if i in any_inputs else arg
                for i, arg in enumerate(args)
            ]
        )

    return run


def spread_kernel(rows, out):
    pieces = [rows[:, k * LANES : (k + 1) * LANES].astype(f32) for k in range(PIECES)]
    stacked = jnp.concatenate([p[0:1, :] for p in pieces] + [p[1:2, :] for p in pieces], axis=0)
    stacked = stacked.astype(bf16)
    for peer in range(PEERS):
        out[peer, :, :] = stacked


def act_kernel(gate_up, codes, out):
    gate = gate_up[0].astype(f32)
    act = (gate / (1.0 + jnp.exp(-gate)) * gate_up[1].astype(f32)).astype(bf16)
    out[...] = dot(sign_rows(codes[...]), act, NN)


def table_kernel(codes, out):
    for block in range(8):
        cols = pl.ds(block * 512, 512)
        out[0:RANK, cols] = sign_rows(codes[0:1, cols])
        out[RANK : 2 * RANK, cols] = sign_rows(codes[1:2, cols])


def norm_pieces(x, gain, xf, hid, normed):
    for peer in range(PEERS):
        rows = slice(peer * 2 * PIECES, (peer + 1) * 2 * PIECES)
        xf[peer * PITCH : peer * PITCH + 2 * PIECES, :] = x[rows, :].astype(f32)
    squares = jnp.zeros((TOK, LANES), f32)
    for k in range(PIECES):
        piece = token_piece(xf, k)
        squares = squares + piece * piece
        hid[:, k * LANES : (k + 1) * LANES] = piece.astype(bf16)
    inv = lax.rsqrt(jnp.sum(squares, axis=1, keepdims=True) * (1.0 / D) + 1e-05)
    for k in range(PIECES):
        cols = slice(k * LANES, (k + 1) * LANES)
        unit = hid[:, cols].astype(f32) * inv
        normed[:, cols] = (unit * gain[k : k + 1, :]).astype(bf16)
    return squares


def score_kernel(x, gain, w_own, w_par, acts, logits, payload, xf, hid, normed, w, sems):
    copies = []
    for block in range(4):
        source = w_own if block < 2 else w_par
        copy = pltpu.make_async_copy(
            source.at[pl.ds((block % 2) * 256, 256)], w.at[pl.ds(block * 256, 256)], sems.at[block]
        )
        copy.start()
        copies.append(copy)
    norm_pieces(x, gain, xf, hid, normed)
    for block in range(4):
        copies[block].wait()
        part = slice(block * 256, (block + 1) * 256)
        logits[part, :] = dot(w[part, :], normed[...], NT)
    scores = logits[...]
    top = jnp.max(scores, axis=0, keepdims=True)
    total = jnp.sum(jnp.exp(scores - top), axis=0, keepdims=True)
    payload[pl.ds(0, PEERS, stride=4), :] = jnp.broadcast_to(top, (PEERS, LANES))
    payload[pl.ds(1, PEERS, stride=4), :] = jnp.broadcast_to(total, (PEERS, LANES))
    payload[pl.ds(2, PEERS, stride=4), :] = acts[...]
    payload[pl.ds(3, PEERS, stride=4), :] = jnp.zeros((PEERS, LANES), f32)


def split(values):
    high = values.astype(bf16)
    return high, (values - high.astype(f32)).astype(bf16)


def backward_kernel(
    logits, hit, codes, table, gain_row, x, gain, w_own, w_par,
    soft_out, picked_out, columns, aux,
    xf, hid, normed, w, soft, picked, w_sems, out_sems,
):
    chunks = D // CHUNK
    copies = []
    for chunk in range(chunks):
        cols = pl.ds(chunk * CHUNK, CHUNK)
        for half, source in enumerate((w_own, w_par)):
            copy = pltpu.make_async_copy(
                source.at[:, cols], w.at[pl.ds(half * VOC, VOC), cols], w_sems.at[chunk, half]
            )
            copy.start()
            copies.append(copy)
    squares = norm_pieces(x, gain, xf, hid, normed)
    sums = jnp.sum(squares.T, axis=0, keepdims=True)
    inv = lax.rsqrt(sums * (1.0 / D) + 1e-05)
    unit_sketch = dot(table[RANK : 2 * RANK, :], hid[...], NT) * inv
    inv = inv * (RANK / D) ** 0.5
    aux[...] = dot(table[0:RANK, :], normed[...], NT) * (RANK / D) ** 0.5
    scores = logits[...]
    top = jnp.max(scores, axis=0, keepdims=True)
    rows = lax.broadcasted_iota(jnp.int32, (2 * VOC, LANES), 0)
    chosen = rows == hit[0:1, :]
    onehot = chosen.astype(f32)
    weights = jnp.exp(scores - top)
    others = jnp.where(chosen, 0.0, weights)
    at_target = jnp.sum(jnp.where(chosen, weights, 0.0), axis=0, keepdims=True)
    at_target_rows = jnp.broadcast_to(at_target, (LANES, LANES)).T
    high, low = split(others)
    left = jnp.concatenate(
        [others.T.astype(bf16), low.astype(f32).T.astype(bf16), onehot.T.astype(bf16)], axis=0
    )
    sums = jnp.zeros((RANK, 4 * TOK), f32)
    outs = []
    for chunk in range(chunks):
        copies[2 * chunk].wait()
        copies[2 * chunk + 1].wait()
        cols = slice(chunk * CHUNK, (chunk + 1) * CHUNK)
        both = dot(left, w[:, cols], NN)
        pick = both[2 * TOK :, :]
        full = both[0:TOK, :] + both[TOK : 2 * TOK, :]
        for k in range(CHUNK // LANES):
            lanes = slice(k * LANES, (k + 1) * LANES)
            place = slice(chunk * CHUNK + k * LANES, chunk * CHUNK + (k + 1) * LANES)
            soft[:, place] = full[:, lanes] + at_target_rows * pick[:, lanes]
        picked[:, cols] = pick.astype(bf16)
        spot = pl.ds(chunk * CHUNK, CHUNK)
        for sem, (source, target) in enumerate(((soft, soft_out), (picked, picked_out))):
            copy = pltpu.make_async_copy(
                source.at[:, spot], target.at[:, spot], out_sems.at[chunk, sem]
            )
            copy.start()
            outs.append(copy)
        full_high, full_low = split(soft[:, cols] * gain_row[:, cols])
        pick_high, pick_low = split(pick * gain_row[:, cols])
        right = jnp.concatenate([full_high, full_low, pick_high, pick_low], axis=0)
        sums = sums + dot(table[RANK : 2 * RANK, cols], right, NT)
    full_sketch = sums[:, 0:TOK] + sums[:, TOK : 2 * TOK]
    pick_sketch = sums[:, 2 * TOK : 3 * TOK] + sums[:, 3 * TOK :]
    full_mean = jnp.sum(weights * scores, axis=0, keepdims=True) * (1.0 / D)
    pick_mean = jnp.sum(onehot * scores, axis=0, keepdims=True) * (1.0 / D)
    signs = sign_rows(codes[...])
    pick_vocab = dot(signs, onehot.astype(bf16), NN)
    soft_vocab = dot(signs, high, NN) + dot(signs, low, NN) + at_target * pick_vocab
    columns[0:RANK, :] = soft_vocab
    columns[RANK : 2 * RANK, :] = pick_vocab
    columns[2 * RANK : 3 * RANK, :] = inv * (full_sketch - unit_sketch * full_mean)
    columns[3 * RANK : 4 * RANK, :] = inv * (pick_sketch - unit_sketch * pick_mean)
    columns[4 * RANK : 4 * RANK + 8, :] = jnp.broadcast_to(top, (8, LANES))
    for copy in outs:
        copy.wait()


def scale_kernel(stats, soft_in, picked_in, columns, blocks, df, soft, picked, sems):
    copies = []
    for chunk in range(D // CHUNK):
        cols = pl.ds(chunk * CHUNK, CHUNK)
        for sem, (source, target) in enumerate(((soft_in, soft), (picked_in, picked))):
            copy = pltpu.make_async_copy(
                source.at[:, cols], target.at[:, cols], sems.at[chunk, sem]
            )
            copy.start()
            copies.append(copy)
    tops = stats[pl.ds(0, PEERS, stride=4), :]
    totals = stats[pl.ds(1, PEERS, stride=4), :]
    acts = jnp.sum(stats[pl.ds(2, PEERS, stride=4), :], axis=0, keepdims=True)
    top = jnp.max(tops, axis=0, keepdims=True)
    denominator = jnp.sum(totals * jnp.exp(tops - top), axis=0, keepdims=True)
    scale = jnp.exp(columns[4 * RANK : 4 * RANK + 1, :] - top) / denominator
    scale_rows = jnp.broadcast_to(scale, (LANES, LANES)).T
    for k in range(PIECES):
        if k % (CHUNK // LANES) == 0:
            chunk = k // (CHUNK // LANES)
            copies[2 * chunk].wait()
            copies[2 * chunk + 1].wait()
        lanes = slice(k * LANES, (k + 1) * LANES)
        piece = scale_rows * soft[:, lanes] - picked[:, lanes].astype(f32)
        df[pl.ds(k, PEERS, stride=PITCH), :] = piece[0:PEERS, :]
        df[pl.ds(PIECES + k, PEERS, stride=PITCH), :] = piece[PEERS:TOK, :]
    vocab_sketch = scale * columns[0:RANK, :] - columns[RANK : 2 * RANK, :]
    grad_sketch = scale * columns[2 * RANK : 3 * RANK, :] - columns[3 * RANK : 4 * RANK, :]
    acts = jnp.broadcast_to(acts, (PEERS, LANES))
    for place, values in enumerate((vocab_sketch, grad_sketch, acts)):
        high = values.astype(bf16).astype(f32)
        df[pl.ds(2 * PIECES + 2 * place, PEERS, stride=PITCH), :] = high
        df[pl.ds(2 * PIECES + 2 * place + 1, PEERS, stride=PITCH), :] = values - high
    for row in (6, 7):
        df[pl.ds(2 * PIECES + row, PEERS, stride=PITCH), :] = jnp.zeros((PEERS, LANES), f32)
    blocks[...] = df[...].reshape(PEERS, PITCH, LANES).astype(bf16)


def feature_kernel(blocks, aux, docs, core, mine, other, rows):
    rows[...] = blocks[...].astype(f32)[:, 2 * PIECES :, :].reshape(PEERS * 8, LANES)

    def row(place):
        return rows[pl.ds(place, PEERS, stride=8), :]

    vocab_column = jnp.sum(row(0) + row(1), axis=0, keepdims=True)
    grad_column = jnp.sum(row(2) + row(3), axis=0, keepdims=True)
    acts = row(4) + row(5)
    act_sketch = jnp.concatenate([acts[:, 0:RANK], acts[:, RANK : 2 * RANK]], axis=0)
    act_sketch = act_sketch * (RANK / FF) ** 0.5
    ids = lax.broadcasted_iota(jnp.int32, (DOCS, LANES), 0)
    member = (docs[0:1, :] == ids).astype(f32)
    high = lax.Precision.HIGHEST
    head = dot(member * vocab_column, aux[...], NT, high)
    down = dot(member * grad_column, act_sketch, NN, high)
    both = jnp.concatenate([head, down], axis=0)
    first, second = both[:, 0 : RANK // 2], both[:, RANK // 2 :]
    is_first = core[0:1, 0:1] == 0
    mine[...] = jnp.where(is_first, first, second)
    other[...] = jnp.where(is_first, second, first)


def resid_kernel(blocks, hidden, gain, out):
    received = blocks[...].astype(f32)
    total = jnp.zeros((2 * PIECES, LANES), f32)
    for source in range(PEERS):
        total = total + received[source, 0 : 2 * PIECES, :]
    grads = []
    for token in range(2):
        rows = slice(token * PIECES, (token + 1) * PIECES)
        values = hidden[rows, :].astype(f32)
        inv = lax.rsqrt(jnp.sum(values * values, keepdims=True) * (1.0 / D) + 1e-05)
        unit = values * inv
        weighted = gain[...] * total[rows, :]
        inner = jnp.sum(weighted * unit, keepdims=True) * (1.0 / D)
        grads.append(inv * (weighted - unit * inner))
    for k in range(PIECES):
        pair = jnp.concatenate([grads[0][k : k + 1, :], grads[1][k : k + 1, :]], axis=0)
        out[:, k * LANES : (k + 1) * LANES] = pair.astype(bf16)


def shards(
    hidden,
    norm_gain,
    head_weight,
    gate_up,
    targets,
    doc_ids,
    vocab_codes,
    hidden_codes,
    model_codes,
):
    index = lax.axis_index("tensor")
    core = lax.rem(index, 2)
    groups = [list(range(0, 2 * PEERS, 2)), list(range(1, 2 * PEERS, 2))]
    partner = [(i, i ^ 1) for i in range(2 * PEERS)]
    gain32 = norm_gain.astype(f32)
    gain_row = gain32.reshape(1, D)
    gain_blk = gain32.reshape(PIECES, LANES)
    own_rows = hidden.reshape(2 * PIECES, LANES)

    def exchange(rows):
        return lax.all_to_all(rows, "tensor", 0, 0, axis_index_groups=groups, tiled=True)

    with jax.named_scope("gather_hidden"):
        spread = call(
            spread_kernel,
            jax.ShapeDtypeStruct((PEERS, 2 * PIECES, LANES), bf16),
            [],
            1,
            1000,
            MIB,
        )(hidden)
        gathered = exchange(spread).reshape(PEERS * 2 * PIECES, LANES)
    with jax.named_scope("partner_rows"):
        w_par = lax.ppermute(head_weight, "tensor", partner)
    with jax.named_scope("activations"):
        act_part = call(act_kernel, jax.ShapeDtypeStruct((RANK, 256), f32), [], 2, 8000000, 300000)(
            gate_up, hidden_codes.reshape(1, -1)
        )
        act_part = act_part.T.reshape(PEERS, 2, LANES)
        act_mine = lax.dynamic_index_in_dim(act_part, core, axis=1, keepdims=False)
        act_other = lax.dynamic_index_in_dim(act_part, 1 - core, axis=1, keepdims=False)
        codes_own = vocab_codes.astype(f32).reshape(VOC // LANES, LANES)
        sent = jnp.concatenate([act_other, codes_own], axis=0)
        came = lax.ppermute(sent, "tensor", partner)
        acts = act_mine + came[:PEERS]
        codes_par = came[PEERS:].astype(jnp.int32).reshape(1, VOC)
        codes = jnp.concatenate([vocab_codes.reshape(1, VOC), codes_par], axis=1)
    with jax.named_scope("tables"):
        table = call(
            table_kernel, jax.ShapeDtypeStruct((2 * RANK, D), bf16), [], 1, 4000000, 1100000
        )(model_codes)
        ids = jnp.stack([targets, doc_ids]).reshape(2, PEERS, 2, 2)
        ids = lax.dynamic_index_in_dim(ids, core, axis=2, keepdims=False)
        ids = ids.transpose(0, 2, 1).reshape(2, TOK)
        relative = ids[0] - index * VOC
        relative_par = ids[0] - (index + 1 - 2 * core) * VOC
        hit = jnp.where(
            (relative >= 0) & (relative < VOC),
            relative,
            jnp.where((relative_par >= 0) & (relative_par < VOC), relative_par + VOC, -1),
        ).reshape(1, TOK)
        docs = ids[1].reshape(1, TOK)
        core_row = jnp.full((1, LANES), core, jnp.int32)

    norm_scratch = [
        pltpu.VMEM((PEERS * PITCH, LANES), f32),
        pltpu.VMEM((TOK, D), bf16),
        pltpu.VMEM((TOK, D), bf16),
    ]
    with jax.named_scope("scores"):
        logits, payload = call(
            score_kernel,
            (
                jax.ShapeDtypeStruct((2 * VOC, TOK), f32),
                jax.ShapeDtypeStruct((PEERS * 4, LANES), f32),
            ),
            norm_scratch + [pltpu.VMEM((2 * VOC, D), bf16), pltpu.SemaphoreType.DMA((4,))],
            5,
            1 << 30,
            10 * MIB,
            any_inputs=(2, 3),
        )(gathered, gain_blk, head_weight, w_par, acts)
    with jax.named_scope("statistics"):
        stats = exchange(payload.reshape(PEERS, 4, LANES)).reshape(PEERS * 4, LANES)
    with jax.named_scope("backward"):
        soft, picked, columns, aux = call(
            backward_kernel,
            (
                jax.ShapeDtypeStruct((TOK, D), f32),
                jax.ShapeDtypeStruct((TOK, D), bf16),
                jax.ShapeDtypeStruct((4 * RANK + 8, LANES), f32),
                jax.ShapeDtypeStruct((RANK, LANES), f32),
            ),
            norm_scratch
            + [
                pltpu.VMEM((2 * VOC, D), bf16),
                pltpu.VMEM((TOK, D), f32),
                pltpu.VMEM((TOK, D), bf16),
                pltpu.SemaphoreType.DMA((D // CHUNK, 2)),
                pltpu.SemaphoreType.DMA((D // CHUNK, 2)),
            ],
            9,
            3 << 30,
            12 * MIB,
            any_inputs=(7, 8),
            any_outs=(0, 1),
        )(logits, hit, codes, table, gain_row, gathered, gain_blk, head_weight, w_par)
    with jax.named_scope("scale"):
        blocks = call(
            scale_kernel,
            jax.ShapeDtypeStruct((PEERS, PITCH, LANES), bf16),
            [
                pltpu.VMEM((PEERS * PITCH, LANES), f32),
                pltpu.VMEM((TOK, D), f32),
                pltpu.VMEM((TOK, D), bf16),
                pltpu.SemaphoreType.DMA((D // CHUNK, 2)),
            ],
            4,
            2000000,
            4 * MIB,
            any_inputs=(1, 2),
        )(stats, soft, picked, columns)
    with jax.named_scope("scatter_dnormed"):
        blocks, docs, core_row, gain_blk, aux, own_rows = lax.optimization_barrier(
            (blocks, docs, core_row, gain_blk, aux, own_rows)
        )
        received = exchange(blocks)
    with jax.named_scope("features"):
        half = jax.ShapeDtypeStruct((2 * DOCS, RANK // 2), f32)
        mine, other = call(
            feature_kernel,
            (half, half),
            [pltpu.VMEM((PEERS * 8, LANES), f32)],
            4,
            2000000,
            300000,
        )(received, aux, docs, core_row)
        features = mine + lax.ppermute(other, "tensor", partner)
    with jax.named_scope("resid_grad"):
        resid = call(
            resid_kernel,
            jax.ShapeDtypeStruct((2, D), bf16),
            [],
            3,
            2000000,
            MIB,
        )(received, own_rows, gain_blk)
    return resid, features[:DOCS], features[DOCS:]


def solution(mesh):
    in_specs = (
        P(("dp", "tensor"), None),
        P(),
        P("tensor", None),
        P(None, "tensor", "dp"),
        P("dp"),
        P("dp"),
        P("tensor"),
        P("tensor"),
        P(),
    )
    out_specs = (P(("dp", "tensor"), None), P("dp", "tensor"), P("dp", "tensor"))
    return jax.shard_map(shards, mesh=mesh, in_specs=in_specs, out_specs=out_specs, check_vma=False)
```

time: 156 us -> 128 us (0.82)
  waiting for transfers between devices: 69.6 us -> 29.6 us
  blocking collectives: 16 us -> 40.9 us
  starting transfers between devices: 39.9 us -> 30.1 us
  local copies, waits for them, and re-layouts: 9.98 us -> 2.39 us
  Pallas kernels: 18.6 us -> 22.6 us
    all_to_all x3 -> x2, waiting for transfers between devices: 58.1 us -> 29.5 us  [exchange(): lax.all_to_all(rows, 'tensor', 0, 0, axis_index_groups=groups, tiled=True)]
    all_to_all x1, blocking collectives: 16 us -> 40.9 us  [exchange(): lax.all_to_all(rows, 'tensor', 0, 0, axis_index_groups=groups, tiled=True)]
    all_to_all x1 -> x0, starting transfers between devices: 17.9 us -> none  [shards(): act_all = lax.all_to_all(act_blocks, 'tensor', 0, 0, tiled=True)]
    all_to_all x1 -> x0, waiting for transfers between devices: 10.4 us -> none  [shards(): act_all = lax.all_to_all(act_blocks, 'tensor', 0, 0, tiled=True)]
    all_to_all x3 -> x2, starting transfers between devices: 16.3 us -> 24 us  [exchange(): lax.all_to_all(rows, 'tensor', 0, 0, axis_index_groups=groups, tiled=True)]
    pallas_call x8, Pallas kernels: 18.6 us -> 22.6 us  [run(): inner(*[pltpu.with_memory_space_constraint(arg, pltpu.HBM) if i in any_in...]
    unnamed x12 -> x18, local copies, waits for them, and re-layouts: 3.81 us -> 0.74 us
    broadcast_in_dim x2 -> x1, local copies, waits for them, and re-layouts: 1.96 us -> 0.01 us  [shards(): core_row = jnp.full((1, LANES), core, jnp.int32)]
  transfers between devices with their start and end apart: 7 -> 5, of which waited for: 5 -> 3; matrix products, arithmetic and copies ran while one was open for 4% -> 1% of each run, Pallas kernels for 7% -> 10%
where the time goes in v2:
time: 128 us; the launch traced here: 126 us
  blocking collectives  40.9 us (32%)
  starting transfers between devices  30.1 us (24%)
  waiting for transfers between devices  29.6 us (23%)
  Pallas kernels  22.6 us (18%)
  local copies, waits for them, and re-layouts  2.39 us (2%)
    all_to_all x1, blocking collectives, exchange(): lax.all_to_all(rows, 'tensor', 0, 0, axis_index_groups=groups, tiled=True)  40.9 us
    all_to_all x2, waiting for transfers between devices, exchange(): lax.all_to_all(rows, 'tensor', 0, 0, axis_index_groups=groups, tiled=True)  29.5 us
    all_to_all x2, starting transfers between devices, exchange(): lax.all_to_all(rows, 'tensor', 0, 0, axis_index_groups=groups, tiled=True)  24 us
    pallas_call x8, Pallas kernels, run(): inner(*[pltpu.with_memory_space_constraint(arg, pltpu.HBM) if i in any_in...  22.6 us
  transfers between devices with their start and end apart: 5, of which 3 were waited for; matrix products, arithmetic and copies ran while one was open for 1% of the time, Pallas kernels for 10%

profile of v2, /device:TPU:6, one launch (start us, length us, event | category | flops | bytes accessed | tf_op | source)
XLA Modules:
  0.0 126.5 jit_solution(5126206008640318676)
XLA Ops:
  0.6 0.0 copy-start
  0.6 2.1 %collective-permute-start = (bf16[512,4096]{1,0:T(8,128)(2,1)}, bf16[512,4096]{1,0:T(8,128)(2,1)}, u32[]{:S(2)}, u32[]{:S(2)}) collective-permute-start(bf16[512,4096]{1,0:T(8,128)(2,1)} %w_own.3), channel_id=1, source_target_pairs={{0,1},{1,0},{2,3},{3,2},{4,5},{5,4},{6,7},{7,6},{8,9},{9,8},{10,11... | collective-permute-start | bytes 12582920 | tf_op jit(solution)/shard_map/partner_rows/ppermute | solution.py:339
  2.7 0.0 copy-start.1
  2.7 0.7 copy-done.1
  3.4 0.0 copy-start.4
  3.4 0.0 copy-start.6
  3.4 0.0 copy-start.7
  3.4 0.0 copy-start.8
  3.4 0.0 copy-start.5
  3.4 0.0 copy-start.2
  3.5 0.0 copy-start.3
  3.5 1.1 gather_hidden.1
  4.6 16.6 %all-to-all-start = ((bf16[64,64,128]{2,1,0:T(8,128)(2,1)}), bf16[64,64,128]{2,1,0:T(8,128)(2,1)S(1)}, u32[]{:S(2)}, u32[]{:S(2)}) async-start(bf16[64,64,128]{2,1,0:T(8,128)(2,1)} %gather_hidden.1), calls=%async_computation | async-start | bytes 2097152 | tf_op jit(solution)/shard_map/gather_hidden/all_to_all | solution.py:326
  21.2 0.0 copy-done
  21.2 0.0 copy-done.4
  21.2 0.2 activations.1
  21.4 0.1 copy.15
  21.5 0.1 reshape.111
  21.6 0.1 constant_dynamic-slice_fusion
  21.7 0.0 copy-done.6
  21.8 2.1 %collective-permute-start.1 = (f32[68,128]{1,0:T(8,128)S(1)}, f32[68,128]{1,0:T(8,128)S(1)}, u32[]{:S(2)}, u32[]{:S(2)}) collective-permute-start(f32[68,128]{1,0:T(8,128)S(1)} %pad_maximum_fusion), channel_id=1, source_target_pairs={{0,1},{1,0},{2,3},{3,2},{4,5},{5,4},{6,7},{7,6},{8,9},{9,8},{10,11... | collective-permute-start | bytes 104456 | tf_op jit(solution)/shard_map/activations/ppermute | solution.py:349
  23.9 0.0 copy-done.7
  23.9 0.2 stack.9
  24.1 0.1 copy.16
  24.2 0.0 copy-done.8
  24.2 0.2 stack.10
  24.3 0.1 copy.17
  24.4 0.1 sub.39
  24.5 0.1 select_n.37
  24.6 0.0 copy-done.5
  24.6 0.0 copy-done.2
  24.7 0.1 slice.27.docs
  24.7 0.0 copy-done.3
  24.7 0.4 tables.1.table
  25.1 0.0 collective-permute-done.1
  25.2 26.3 %all-to-all-done = bf16[64,64,128]{2,1,0:T(8,128)(2,1)S(1)} async-done(((bf16[64,64,128]{2,1,0:T(8,128)(2,1)}), bf16[64,64,128]{2,1,0:T(8,128)(2,1)S(1)}, u32[]{:S(2)}, u32[]{:S(2)}) %all-to-all-start) | async-done | bytes 1048608 | tf_op jit(solution)/shard_map/gather_hidden/all_to_all | solution.py:326
  51.5 0.0 collective-permute-done.w_par
  51.5 7.8 %scores.1 = (f32[1024,128]{1,0:T(8,128)S(1)}, f32[256,128]{1,0:T(8,128)}) custom-call(bf16[4096,128]{1,0:T(8,128)(2,1)S(1)} %bitcast.18, f32[32,128]{1,0:T(8,128)S(1)} %get-tuple-element.25.gain, bf16[512,4096]{1,0:T(8,128)(2,1)} %w_own.3, bf16[512,4096]{1,0:T(8,128)(2,1)} %collective-permute-done.w_par, f32[64,128]{1,0:T(8,128)S(1)} %slice_add_fusion.acts), custom_call_target="tpu_custom_call" | custom-call | flops 1073741824 | bytes 10485760 | tf_op jit(solution)/shard_map/scores/pallas_call | solution.py:74
  59.3 7.4 %all-to-all-start.1 = ((f32[64,4,128]{2,1,0:T(4,128)}), f32[64,4,128]{2,1,0:T(4,128)S(1)}, u32[]{:S(2)}, u32[]{:S(2)}) async-start(f32[64,4,128]{2,1,0:T(4,128)} %bitcast.7), calls=%async_computation.1 | async-start | bytes 262144 | tf_op jit(solution)/shard_map/statistics/all_to_all | solution.py:326
  66.7 9.4 %backward.1 = (f32[128,4096]{1,0:T(8,128)}, bf16[128,4096]{1,0:T(8,128)(2,1)}, f32[264,128]{1,0:T(8,128)S(1)}, f32[64,128]{1,0:T(8,128)S(1)}) custom-call(f32[1024,128]{1,0:T(8,128)S(1)} %get-tuple-element.18.logits, s32[1,128]{1,0:T(1,128)S(1)} %and_select_fusion.1.hit, s32[1,1024]{1,0:T(1,128)S(1)} %pad_add_fusion.codes, ...), custom_call_target="tpu_custom_call" | custom-call | flops 3221225472 | bytes 12582912 | tf_op jit(solution)/shard_map/backward/pallas_call | solution.py:74
  76.1 3.2 %all-to-all-done.1 = f32[64,4,128]{2,1,0:T(4,128)S(1)} async-done(((f32[64,4,128]{2,1,0:T(4,128)}), f32[64,4,128]{2,1,0:T(4,128)S(1)}, u32[]{:S(2)}, u32[]{:S(2)}) %all-to-all-start.1) | async-done | bytes 131104 | tf_op jit(solution)/shard_map/statistics/all_to_all | solution.py:326
  79.2 2.3 %scale.1 = bf16[64,72,128]{2,1,0:T(8,128)(2,1)S(1)} custom-call(f32[256,128]{1,0:T(8,128)S(1)} %bitcast.20, f32[128,4096]{1,0:T(8,128)} %get-tuple-element.19.soft_in, bf16[128,4096]{1,0:T(8,128)(2,1)} %get-tuple-element.20.picked_in, f32[264,128]{1,0:T(8,128)S(1)} %get-tuple-element.21.columns), custom_call_target="tpu_custom_call" | custom-call | flops 2000000 | bytes 4194304 | tf_op jit(solution)/shard_map/scale/pallas_call | solution.py:74
  81.5 40.9 %all_to_all.15.blocks = bf16[64,72,128]{2,1,0:T(8,128)(2,1)S(1)} all-to-all(bf16[64,72,128]{2,1,0:T(8,128)(2,1)S(1)} %scale.1), channel_id=1, replica_groups={{0,2,4,6,8,10,12,14,16,18,20,22,24,26,28,30,32,34,36,38,40,42,44,46,48,..., dimensions={0} | all-to-all | bytes 2359296 | tf_op jit(solution)/shard_map/scatter_dnormed/all_to_all | solution.py:326
  122.4 0.4 features.1
  122.8 1.9 %collective-permute-start.2 = (f32[16,32]{1,0:T(8,128)S(1)}, f32[16,32]{1,0:T(8,128)S(1)}, u32[]{:S(2)}, u32[]{:S(2)}) collective-permute-start(f32[16,32]{1,0:T(8,128)S(1)} %get-tuple-element.30), channel_id=1, source_target_pairs={{0,1},{1,0},{2,3},{3,2},{4,5},{5,4},{6,7},{7,6},{8,9},{9,8},{10,11... | collective-permute-start | bytes 6152 | tf_op jit(solution)/shard_map/features/ppermute | solution.py:443
  124.7 1.0 resid_grad.1
  125.8 0.1 collective-permute-done.2
  125.9 0.6 fusion.2
  (12 shorter events, 0.1 us)
Async XLA Ops:
  0.6 20.6 %copy-start = (bf16[2,224,256]{2,1,0:T(8,128)(2,1)S(1)}, bf16[2,224,256]{2,1,0:T(8,128)(2,1)}, u32[]{:S(2)}) copy-start(bf16[2,224,256]{2,1,0:T(8,128)(2,1)} %gate_up.1) | copy-start | bytes 688132
  0.6 50.9 %collective-permute-start = (bf16[512,4096]{1,0:T(8,128)(2,1)}, bf16[512,4096]{1,0:T(8,128)(2,1)}, u32[]{:S(2)}, u32[]{:S(2)}) collective-permute-start(bf16[512,4096]{1,0:T(8,128)(2,1)} %w_own.3), channel_id=1, source_target_pairs={{0,1},{1,0},{2,3},{3,2},{4,5},{5,4},{6,7},{7,6},{8,9},{9,8},{10,11... | collective-permute-start | bytes 12582920 | tf_op jit(solution)/shard_map/partner_rows/ppermute | solution.py:339
  2.7 0.7 copy-start.1
  3.4 17.8 %copy-start.4 = (s32[224]{0:T(256)S(1)}, s32[224]{0:T(256)}, u32[]{:S(2)}) copy-start(s32[224]{0:T(256)} %param.16) | copy-start | bytes 2692
  3.4 18.3 %copy-start.6 = (s32[512]{0:T(512)S(1)}, s32[512]{0:T(512)}, u32[]{:S(2)}) copy-start(s32[512]{0:T(512)} %param.15) | copy-start | bytes 6148
  3.4 20.5 %copy-start.7 = (s32[256]{0:T(256)S(1)}, s32[256]{0:T(256)}, u32[]{:S(2)}) copy-start(s32[256]{0:T(256)} %param.13) | copy-start | bytes 3076
  3.4 20.7 %copy-start.8 = (s32[256]{0:T(256)S(1)}, s32[256]{0:T(256)}, u32[]{:S(2)}) copy-start(s32[256]{0:T(256)} %param.14) | copy-start | bytes 3076
  3.4 21.2 %copy-start.5 = (bf16[4096]{0:T(1024)(128)(2,1)S(1)}, bf16[4096]{0:T(1024)(128)(2,1)}, u32[]{:S(2)}) copy-start(bf16[4096]{0:T(1024)(128)(2,1)} %param.10) | copy-start | bytes 24580
  3.4 21.2 %copy-start.2 = (bf16[2,4096]{1,0:T(2,128)(2,1)S(1)}, bf16[2,4096]{1,0:T(2,128)(2,1)}, u32[]{:S(2)}) copy-start(bf16[2,4096]{1,0:T(2,128)(2,1)} %rows.1) | copy-start | bytes 49156
  3.5 21.3 %copy-start.3 = (s32[2,4096]{1,0:T(2,128)S(1)}, s32[2,4096]{1,0:T(2,128)}, u32[]{:S(2)}) copy-start(s32[2,4096]{1,0:T(2,128)} %codes.1) | copy-start | bytes 98308
  4.6 46.9 %all-to-all-start = ((bf16[64,64,128]{2,1,0:T(8,128)(2,1)}), bf16[64,64,128]{2,1,0:T(8,128)(2,1)S(1)}, u32[]{:S(2)}, u32[]{:S(2)}) async-start(bf16[64,64,128]{2,1,0:T(8,128)(2,1)} %gather_hidden.1), calls=%async_computation | async-start | bytes 2097152 | tf_op jit(solution)/shard_map/gather_hidden/all_to_all | solution.py:326
  21.8 3.4 %collective-permute-start.1 = (f32[68,128]{1,0:T(8,128)S(1)}, f32[68,128]{1,0:T(8,128)S(1)}, u32[]{:S(2)}, u32[]{:S(2)}) collective-permute-start(f32[68,128]{1,0:T(8,128)S(1)} %pad_maximum_fusion), channel_id=1, source_target_pairs={{0,1},{1,0},{2,3},{3,2},{4,5},{5,4},{6,7},{7,6},{8,9},{9,8},{10,11... | collective-permute-start | bytes 104456 | tf_op jit(solution)/shard_map/activations/ppermute | solution.py:349
  59.3 20.0 %all-to-all-start.1 = ((f32[64,4,128]{2,1,0:T(4,128)}), f32[64,4,128]{2,1,0:T(4,128)S(1)}, u32[]{:S(2)}, u32[]{:S(2)}) async-start(f32[64,4,128]{2,1,0:T(4,128)} %bitcast.7), calls=%async_computation.1 | async-start | bytes 262144 | tf_op jit(solution)/shard_map/statistics/all_to_all | solution.py:326
  122.8 3.1 %collective-permute-start.2 = (f32[16,32]{1,0:T(8,128)S(1)}, f32[16,32]{1,0:T(8,128)S(1)}, u32[]{:S(2)}, u32[]{:S(2)}) collective-permute-start(f32[16,32]{1,0:T(8,128)S(1)} %get-tuple-element.30), channel_id=1, source_target_pairs={{0,1},{1,0},{2,3},{3,2},{4,5},{5,4},{6,7},{7,6},{8,9},{9,8},{10,11... | collective-permute-start | bytes 6152 | tf_op jit(solution)/shard_map/features/ppermute | solution.py:443

commit v3 on v2

--- a/solution.py
+++ b/solution.py
@@ -15,7 +15,7 @@
 VOC = 512
 FF = 28672
 PITCH = 2 * PIECES + 8
-CHUNK = 512
+CHUNK = 1024
 MIB = 1 << 20
 
 f32 = jnp.float32
@@ -120,19 +120,17 @@
 
 
 def score_kernel(x, gain, w_own, w_par, acts, logits, payload, xf, hid, normed, w, sems):
-    copies = []
-    for block in range(4):
-        source = w_own if block < 2 else w_par
-        copy = pltpu.make_async_copy(
-            source.at[pl.ds((block % 2) * 256, 256)], w.at[pl.ds(block * 256, 256)], sems.at[block]
-        )
-        copy.start()
-        copies.append(copy)
+    copies = [
+        pltpu.make_async_copy(source, w.at[pl.ds(half * VOC, VOC)], sems.at[half])
+        for half, source in enumerate((w_own, w_par))
+    ]
+    copies[0].start()
     norm_pieces(x, gain, xf, hid, normed)
-    for block in range(4):
-        copies[block].wait()
-        part = slice(block * 256, (block + 1) * 256)
-        logits[part, :] = dot(w[part, :], normed[...], NT)
+    copies[1].start()
+    for half in range(2):
+        copies[half].wait()
+        part = slice(half * VOC, (half + 1) * VOC)
+        logits[part, :] = dot(normed[...], w[part, :], NT).T
     scores = logits[...]
     top = jnp.max(scores, axis=0, keepdims=True)
     total = jnp.sum(jnp.exp(scores - top), axis=0, keepdims=True)
@@ -157,11 +155,13 @@
     for chunk in range(chunks):
         cols = pl.ds(chunk * CHUNK, CHUNK)
         for half, source in enumerate((w_own, w_par)):
-            copy = pltpu.make_async_copy(
-                source.at[:, cols], w.at[pl.ds(half * VOC, VOC), cols], w_sems.at[chunk, half]
+            copies.append(
+                pltpu.make_async_copy(
+                    source.at[:, cols], w.at[pl.ds(half * VOC, VOC), cols], w_sems.at[chunk, half]
+                )
             )
-            copy.start()
-            copies.append(copy)
+    for copy in copies:
+        copy.start()
     squares = norm_pieces(x, gain, xf, hid, normed)
     sums = jnp.sum(squares.T, axis=0, keepdims=True)
     inv = lax.rsqrt(sums * (1.0 / D) + 1e-05)
@@ -379,7 +379,7 @@
                 jax.ShapeDtypeStruct((2 * VOC, TOK), f32),
                 jax.ShapeDtypeStruct((PEERS * 4, LANES), f32),
             ),
-            norm_scratch + [pltpu.VMEM((2 * VOC, D), bf16), pltpu.SemaphoreType.DMA((4,))],
+            norm_scratch + [pltpu.VMEM((2 * VOC, D), bf16), pltpu.SemaphoreType.DMA((2,))],
             5,
             1 << 30,
             10 * MIB,

time: 128 us -> 126 us (0.984)
  Pallas kernels: 22.6 us -> 20.6 us
    pallas_call x8, Pallas kernels: 22.6 us -> 20.6 us  [run(): inner(*[pltpu.with_memory_space_constraint(arg, pltpu.HBM) if i in any_in...]
  transfers between devices with their start and end apart: 5 -> 5, of which waited for: 3 -> 3; matrix products, arithmetic and copies ran while one was open for 1% -> 1% of each run, Pallas kernels for 10% -> 9%
where the time goes in v3:
time: 126 us; the launch traced here: 125 us
  blocking collectives  40 us (32%)
  waiting for transfers between devices  30.5 us (24%)
  starting transfers between devices  30.1 us (24%)
  Pallas kernels  20.6 us (16%)
  local copies, waits for them, and re-layouts  2.39 us (2%)
    all_to_all x1, blocking collectives, exchange(): lax.all_to_all(rows, 'tensor', 0, 0, axis_index_groups=groups, tiled=True)  40 us
    all_to_all x2, waiting for transfers between devices, exchange(): lax.all_to_all(rows, 'tensor', 0, 0, axis_index_groups=groups, tiled=True)  30.4 us
    all_to_all x2, starting transfers between devices, exchange(): lax.all_to_all(rows, 'tensor', 0, 0, axis_index_groups=groups, tiled=True)  24 us
    pallas_call x8, Pallas kernels, run(): inner(*[pltpu.with_memory_space_constraint(arg, pltpu.HBM) if i in any_in...  20.6 us
  transfers between devices with their start and end apart: 5, of which 3 were waited for; matrix products, arithmetic and copies ran while one was open for 1% of the time, Pallas kernels for 9%

profile of v3, /device:TPU:6, one launch (start us, length us, event | category | flops | bytes accessed | tf_op | source)
XLA Modules:
  0.0 124.5 jit_solution(17207388262801694823)
XLA Ops:
  0.6 0.0 copy-start
  0.6 2.1 %collective-permute-start = (bf16[512,4096]{1,0:T(8,128)(2,1)}, bf16[512,4096]{1,0:T(8,128)(2,1)}, u32[]{:S(2)}, u32[]{:S(2)}) collective-permute-start(bf16[512,4096]{1,0:T(8,128)(2,1)} %w_own.3), channel_id=1, source_target_pairs={{0,1},{1,0},{2,3},{3,2},{4,5},{5,4},{6,7},{7,6},{8,9},{9,8},{10,11... | collective-permute-start | bytes 12582920 | tf_op jit(solution)/shard_map/partner_rows/ppermute | solution.py:339
  2.7 0.0 copy-start.1
  2.7 0.7 copy-done.1
  3.4 0.0 copy-start.4
  3.4 0.0 copy-start.6
  3.4 0.0 copy-start.7
  3.4 0.0 copy-start.8
  3.4 0.0 copy-start.5
  3.4 0.0 copy-start.2
  3.5 0.0 copy-start.3
  3.5 1.1 gather_hidden.1
  4.6 16.6 %all-to-all-start = ((bf16[64,64,128]{2,1,0:T(8,128)(2,1)}), bf16[64,64,128]{2,1,0:T(8,128)(2,1)S(1)}, u32[]{:S(2)}, u32[]{:S(2)}) async-start(bf16[64,64,128]{2,1,0:T(8,128)(2,1)} %gather_hidden.1), calls=%async_computation | async-start | bytes 2097152 | tf_op jit(solution)/shard_map/gather_hidden/all_to_all | solution.py:326
  21.2 0.0 copy-done
  21.2 0.0 copy-done.4
  21.2 0.2 activations.1
  21.4 0.1 copy.15
  21.5 0.1 reshape.111
  21.6 0.1 constant_dynamic-slice_fusion
  21.7 0.0 copy-done.6
  21.8 2.1 %collective-permute-start.1 = (f32[68,128]{1,0:T(8,128)S(1)}, f32[68,128]{1,0:T(8,128)S(1)}, u32[]{:S(2)}, u32[]{:S(2)}) collective-permute-start(f32[68,128]{1,0:T(8,128)S(1)} %pad_maximum_fusion), channel_id=1, source_target_pairs={{0,1},{1,0},{2,3},{3,2},{4,5},{5,4},{6,7},{7,6},{8,9},{9,8},{10,11... | collective-permute-start | bytes 104456 | tf_op jit(solution)/shard_map/activations/ppermute | solution.py:349
  23.9 0.0 copy-done.7
  23.9 0.2 stack.9
  24.1 0.1 copy.16
  24.2 0.0 copy-done.8
  24.2 0.2 stack.10
  24.3 0.1 copy.17
  24.4 0.1 sub.39
  24.5 0.1 select_n.37
  24.6 0.0 copy-done.5
  24.6 0.0 copy-done.2
  24.7 0.1 slice.27.docs
  24.7 0.0 copy-done.3
  24.7 0.4 tables.1.table
  25.1 0.0 collective-permute-done.1
  25.2 26.3 %all-to-all-done = bf16[64,64,128]{2,1,0:T(8,128)(2,1)S(1)} async-done(((bf16[64,64,128]{2,1,0:T(8,128)(2,1)}), bf16[64,64,128]{2,1,0:T(8,128)(2,1)S(1)}, u32[]{:S(2)}, u32[]{:S(2)}) %all-to-all-start) | async-done | bytes 1048608 | tf_op jit(solution)/shard_map/gather_hidden/all_to_all | solution.py:326
  51.5 0.0 collective-permute-done.w_par
  51.5 6.7 %scores.1 = (f32[1024,128]{1,0:T(8,128)S(1)}, f32[256,128]{1,0:T(8,128)}) custom-call(bf16[4096,128]{1,0:T(8,128)(2,1)S(1)} %bitcast.18, f32[32,128]{1,0:T(8,128)S(1)} %get-tuple-element.25.gain, bf16[512,4096]{1,0:T(8,128)(2,1)} %w_own.3, bf16[512,4096]{1,0:T(8,128)(2,1)} %collective-permute-done.w_par, f32[64,128]{1,0:T(8,128)S(1)} %slice_add_fusion.acts), custom_call_target="tpu_custom_call" | custom-call | flops 1073741824 | bytes 10485760 | tf_op jit(solution)/shard_map/scores/pallas_call | solution.py:74
  58.2 7.4 %all-to-all-start.1 = ((f32[64,4,128]{2,1,0:T(4,128)}), f32[64,4,128]{2,1,0:T(4,128)S(1)}, u32[]{:S(2)}, u32[]{:S(2)}) async-start(f32[64,4,128]{2,1,0:T(4,128)} %bitcast.7), calls=%async_computation.1 | async-start | bytes 262144 | tf_op jit(solution)/shard_map/statistics/all_to_all | solution.py:326
  65.6 8.5 %backward.1 = (f32[128,4096]{1,0:T(8,128)}, bf16[128,4096]{1,0:T(8,128)(2,1)}, f32[264,128]{1,0:T(8,128)S(1)}, f32[64,128]{1,0:T(8,128)S(1)}) custom-call(f32[1024,128]{1,0:T(8,128)S(1)} %get-tuple-element.18.logits, s32[1,128]{1,0:T(1,128)S(1)} %and_select_fusion.1.hit, s32[1,1024]{1,0:T(1,128)S(1)} %pad_add_fusion.codes, ...), custom_call_target="tpu_custom_call" | custom-call | flops 3221225472 | bytes 12582912 | tf_op jit(solution)/shard_map/backward/pallas_call | solution.py:74
  74.1 4.1 %all-to-all-done.1 = f32[64,4,128]{2,1,0:T(4,128)S(1)} async-done(((f32[64,4,128]{2,1,0:T(4,128)}), f32[64,4,128]{2,1,0:T(4,128)S(1)}, u32[]{:S(2)}, u32[]{:S(2)}) %all-to-all-start.1) | async-done | bytes 131104 | tf_op jit(solution)/shard_map/statistics/all_to_all | solution.py:326
  78.2 2.2 %scale.1 = bf16[64,72,128]{2,1,0:T(8,128)(2,1)S(1)} custom-call(f32[256,128]{1,0:T(8,128)S(1)} %bitcast.20, f32[128,4096]{1,0:T(8,128)} %get-tuple-element.19.soft_in, bf16[128,4096]{1,0:T(8,128)(2,1)} %get-tuple-element.20.picked_in, f32[264,128]{1,0:T(8,128)S(1)} %get-tuple-element.21.columns), custom_call_target="tpu_custom_call" | custom-call | flops 2000000 | bytes 4194304 | tf_op jit(solution)/shard_map/scale/pallas_call | solution.py:74
  80.4 40.0 %all_to_all.15.blocks = bf16[64,72,128]{2,1,0:T(8,128)(2,1)S(1)} all-to-all(bf16[64,72,128]{2,1,0:T(8,128)(2,1)S(1)} %scale.1), channel_id=1, replica_groups={{0,2,4,6,8,10,12,14,16,18,20,22,24,26,28,30,32,34,36,38,40,42,44,46,48,..., dimensions={0} | all-to-all | bytes 2359296 | tf_op jit(solution)/shard_map/scatter_dnormed/all_to_all | solution.py:326
  120.4 0.4 features.1
  120.8 1.9 %collective-permute-start.2 = (f32[16,32]{1,0:T(8,128)S(1)}, f32[16,32]{1,0:T(8,128)S(1)}, u32[]{:S(2)}, u32[]{:S(2)}) collective-permute-start(f32[16,32]{1,0:T(8,128)S(1)} %get-tuple-element.30), channel_id=1, source_target_pairs={{0,1},{1,0},{2,3},{3,2},{4,5},{5,4},{6,7},{7,6},{8,9},{9,8},{10,11... | collective-permute-start | bytes 6152 | tf_op jit(solution)/shard_map/features/ppermute | solution.py:443
  122.8 1.0 resid_grad.1
  123.8 0.1 collective-permute-done.2
  123.9 0.6 fusion.2
  (12 shorter events, 0.1 us)
Async XLA Ops:
  0.6 20.6 %copy-start = (bf16[2,224,256]{2,1,0:T(8,128)(2,1)S(1)}, bf16[2,224,256]{2,1,0:T(8,128)(2,1)}, u32[]{:S(2)}) copy-start(bf16[2,224,256]{2,1,0:T(8,128)(2,1)} %gate_up.1) | copy-start | bytes 688132
  0.6 50.9 %collective-permute-start = (bf16[512,4096]{1,0:T(8,128)(2,1)}, bf16[512,4096]{1,0:T(8,128)(2,1)}, u32[]{:S(2)}, u32[]{:S(2)}) collective-permute-start(bf16[512,4096]{1,0:T(8,128)(2,1)} %w_own.3), channel_id=1, source_target_pairs={{0,1},{1,0},{2,3},{3,2},{4,5},{5,4},{6,7},{7,6},{8,9},{9,8},{10,11... | collective-permute-start | bytes 12582920 | tf_op jit(solution)/shard_map/partner_rows/ppermute | solution.py:339
  2.7 0.7 copy-start.1
  3.4 17.8 %copy-start.4 = (s32[224]{0:T(256)S(1)}, s32[224]{0:T(256)}, u32[]{:S(2)}) copy-start(s32[224]{0:T(256)} %param.16) | copy-start | bytes 2692
  3.4 18.3 %copy-start.6 = (s32[512]{0:T(512)S(1)}, s32[512]{0:T(512)}, u32[]{:S(2)}) copy-start(s32[512]{0:T(512)} %param.15) | copy-start | bytes 6148
  3.4 20.5 %copy-start.7 = (s32[256]{0:T(256)S(1)}, s32[256]{0:T(256)}, u32[]{:S(2)}) copy-start(s32[256]{0:T(256)} %param.13) | copy-start | bytes 3076
  3.4 20.7 %copy-start.8 = (s32[256]{0:T(256)S(1)}, s32[256]{0:T(256)}, u32[]{:S(2)}) copy-start(s32[256]{0:T(256)} %param.14) | copy-start | bytes 3076
  3.4 21.2 %copy-start.5 = (bf16[4096]{0:T(1024)(128)(2,1)S(1)}, bf16[4096]{0:T(1024)(128)(2,1)}, u32[]{:S(2)}) copy-start(bf16[4096]{0:T(1024)(128)(2,1)} %param.10) | copy-start | bytes 24580
  3.4 21.2 %copy-start.2 = (bf16[2,4096]{1,0:T(2,128)(2,1)S(1)}, bf16[2,4096]{1,0:T(2,128)(2,1)}, u32[]{:S(2)}) copy-start(bf16[2,4096]{1,0:T(2,128)(2,1)} %rows.1) | copy-start | bytes 49156
  3.5 21.3 %copy-start.3 = (s32[2,4096]{1,0:T(2,128)S(1)}, s32[2,4096]{1,0:T(2,128)}, u32[]{:S(2)}) copy-start(s32[2,4096]{1,0:T(2,128)} %codes.1) | copy-start | bytes 98308
  4.6 46.9 %all-to-all-start = ((bf16[64,64,128]{2,1,0:T(8,128)(2,1)}), bf16[64,64,128]{2,1,0:T(8,128)(2,1)S(1)}, u32[]{:S(2)}, u32[]{:S(2)}) async-start(bf16[64,64,128]{2,1,0:T(8,128)(2,1)} %gather_hidden.1), calls=%async_computation | async-start | bytes 2097152 | tf_op jit(solution)/shard_map/gather_hidden/all_to_all | solution.py:326
  21.8 3.4 %collective-permute-start.1 = (f32[68,128]{1,0:T(8,128)S(1)}, f32[68,128]{1,0:T(8,128)S(1)}, u32[]{:S(2)}, u32[]{:S(2)}) collective-permute-start(f32[68,128]{1,0:T(8,128)S(1)} %pad_maximum_fusion), channel_id=1, source_target_pairs={{0,1},{1,0},{2,3},{3,2},{4,5},{5,4},{6,7},{7,6},{8,9},{9,8},{10,11... | collective-permute-start | bytes 104456 | tf_op jit(solution)/shard_map/activations/ppermute | solution.py:349
  58.2 20.0 %all-to-all-start.1 = ((f32[64,4,128]{2,1,0:T(4,128)}), f32[64,4,128]{2,1,0:T(4,128)S(1)}, u32[]{:S(2)}, u32[]{:S(2)}) async-start(f32[64,4,128]{2,1,0:T(4,128)} %bitcast.7), calls=%async_computation.1 | async-start | bytes 262144 | tf_op jit(solution)/shard_map/statistics/all_to_all | solution.py:326
  120.8 3.1 %collective-permute-start.2 = (f32[16,32]{1,0:T(8,128)S(1)}, f32[16,32]{1,0:T(8,128)S(1)}, u32[]{:S(2)}, u32[]{:S(2)}) collective-permute-start(f32[16,32]{1,0:T(8,128)S(1)} %get-tuple-element.30), channel_id=1, source_target_pairs={{0,1},{1,0},{2,3},{3,2},{4,5},{5,4},{6,7},{7,6},{8,9},{9,8},{10,11... | collective-permute-start | bytes 6152 | tf_op jit(solution)/shard_map/features/ppermute | solution.py:443

commit v4 on v3

--- a/solution.py
+++ b/solution.py
@@ -16,6 +16,7 @@
 FF = 28672
 PITCH = 2 * PIECES + 8
 CHUNK = 1024
+PARTS = 4
 MIB = 1 << 20
 
 f32 = jnp.float32
@@ -119,16 +120,21 @@
     return squares
 
 
-def score_kernel(x, gain, w_own, w_par, acts, logits, payload, xf, hid, normed, w, sems):
-    copies = [
-        pltpu.make_async_copy(source, w.at[pl.ds(half * VOC, VOC)], sems.at[half])
-        for half, source in enumerate((w_own, w_par))
-    ]
-    copies[0].start()
+def score_kernel(x, gain, acts, w_own, *refs):
+    w_par, (logits, payload, xf, hid, normed, w, sems) = refs[:PARTS], refs[PARTS:]
+    size = VOC // PARTS
+    copies = [[pltpu.make_async_copy(w_own, w.at[pl.ds(0, VOC)], sems.at[PARTS])], []]
+    for part, source in enumerate(w_par):
+        copies[1].append(
+            pltpu.make_async_copy(source, w.at[pl.ds(VOC + part * size, size)], sems.at[part])
+        )
+    copies[0][0].start()
     norm_pieces(x, gain, xf, hid, normed)
-    copies[1].start()
+    for copy in copies[1]:
+        copy.start()
     for half in range(2):
-        copies[half].wait()
+        for copy in copies[half]:
+            copy.wait()
         part = slice(half * VOC, (half + 1) * VOC)
         logits[part, :] = dot(normed[...], w[part, :], NT).T
     scores = logits[...]
@@ -145,23 +151,27 @@
     return high, (values - high.astype(f32)).astype(bf16)
 
 
-def backward_kernel(
-    logits, hit, codes, table, gain_row, x, gain, w_own, w_par,
-    soft_out, picked_out, columns, aux,
-    xf, hid, normed, w, soft, picked, w_sems, out_sems,
-):
+def backward_kernel(logits, hit, codes, table, gain_row, x, gain, w_own, *refs):
+    w_par, refs = refs[:PARTS], refs[PARTS:]
+    soft_out, picked_out, columns, aux, xf, hid, normed, w, soft, picked, w_sems, out_sems = refs
     chunks = D // CHUNK
+    size = VOC // PARTS
     copies = []
     for chunk in range(chunks):
         cols = pl.ds(chunk * CHUNK, CHUNK)
-        for half, source in enumerate((w_own, w_par)):
-            copies.append(
+        sources = [(w_own, 0, VOC)]
+        sources += [(source, VOC + part * size, size) for part, source in enumerate(w_par)]
+        copies.append(
+            [
                 pltpu.make_async_copy(
-                    source.at[:, cols], w.at[pl.ds(half * VOC, VOC), cols], w_sems.at[chunk, half]
+                    source.at[:, cols], w.at[pl.ds(first, count), cols], w_sems.at[chunk, place]
                 )
-            )
-    for copy in copies:
-        copy.start()
+                for place, (source, first, count) in enumerate(sources)
+            ]
+        )
+    for step in copies:
+        for copy in step:
+            copy.start()
     squares = norm_pieces(x, gain, xf, hid, normed)
     sums = jnp.sum(squares.T, axis=0, keepdims=True)
     inv = lax.rsqrt(sums * (1.0 / D) + 1e-05)
@@ -184,8 +194,8 @@
     sums = jnp.zeros((RANK, 4 * TOK), f32)
     outs = []
     for chunk in range(chunks):
-        copies[2 * chunk].wait()
-        copies[2 * chunk + 1].wait()
+        for copy in copies[chunk]:
+            copy.wait()
         cols = slice(chunk * CHUNK, (chunk + 1) * CHUNK)
         both = dot(left, w[:, cols], NN)
         pick = both[2 * TOK :, :]
@@ -336,7 +346,11 @@
         )(hidden)
         gathered = exchange(spread).reshape(PEERS * 2 * PIECES, LANES)
     with jax.named_scope("partner_rows"):
-        w_par = lax.ppermute(head_weight, "tensor", partner)
+        size = VOC // PARTS
+        w_par = [
+            lax.ppermute(head_weight[part * size : (part + 1) * size], "tensor", partner)
+            for part in range(PARTS)
+        ]
     with jax.named_scope("activations"):
         act_part = call(act_kernel, jax.ShapeDtypeStruct((RANK, 256), f32), [], 2, 8000000, 300000)(
             gate_up, hidden_codes.reshape(1, -1)
@@ -379,12 +393,12 @@
                 jax.ShapeDtypeStruct((2 * VOC, TOK), f32),
                 jax.ShapeDtypeStruct((PEERS * 4, LANES), f32),
             ),
-            norm_scratch + [pltpu.VMEM((2 * VOC, D), bf16), pltpu.SemaphoreType.DMA((2,))],
-            5,
+            norm_scratch + [pltpu.VMEM((2 * VOC, D), bf16), pltpu.SemaphoreType.DMA((PARTS + 1,))],
+            4 + PARTS,
             1 << 30,
             10 * MIB,
-            any_inputs=(2, 3),
-        )(gathered, gain_blk, head_weight, w_par, acts)
+            any_inputs=range(3, 4 + PARTS),
+        )(gathered, gain_blk, acts, head_weight, *w_par)
     with jax.named_scope("statistics"):
         stats = exchange(payload.reshape(PEERS, 4, LANES)).reshape(PEERS * 4, LANES)
     with jax.named_scope("backward"):
@@ -401,15 +415,15 @@
                 pltpu.VMEM((2 * VOC, D), bf16),
                 pltpu.VMEM((TOK, D), f32),
                 pltpu.VMEM((TOK, D), bf16),
-                pltpu.SemaphoreType.DMA((D // CHUNK, 2)),
+                pltpu.SemaphoreType.DMA((D // CHUNK, PARTS + 1)),
                 pltpu.SemaphoreType.DMA((D // CHUNK, 2)),
             ],
-            9,
+            8 + PARTS,
             3 << 30,
             12 * MIB,
-            any_inputs=(7, 8),
+            any_inputs=range(7, 8 + PARTS),
             any_outs=(0, 1),
-        )(logits, hit, codes, table, gain_row, gathered, gain_blk, head_weight, w_par)
+        )(logits, hit, codes, table, gain_row, gathered, gain_blk, head_weight, *w_par)
     with jax.named_scope("scale"):
         blocks = call(
             scale_kernel,

time: 126 us -> 123 us (0.976)
  waiting for transfers between devices: 30.5 us -> 16.6 us
  starting transfers between devices: 30.1 us -> 35.8 us
  local copies, waits for them, and re-layouts: 2.39 us -> 6.79 us
    all_to_all x2, waiting for transfers between devices: 30.4 us -> 14.8 us  [exchange(): lax.all_to_all(rows, 'tensor', 0, 0, axis_index_groups=groups, tiled=True)]
    ppermute x1 -> x4, starting transfers between devices: 2.06 us -> 8.65 us  [shards(): lax.ppermute(head_weight[part * size:(part + 1) * size], 'tensor', partner)]
    slice x0 -> x1, local copies, waits for them, and re-layouts: none -> 4.35 us  [shards(): head_weight[part * size:(part + 1) * size]]
    ppermute x1 -> x4, waiting for transfers between devices: 0.01 us -> 1.65 us  [shards(): lax.ppermute(head_weight[part * size:(part + 1) * size], 'tensor', partner)]
  transfers between devices with their start and end apart: 5 -> 8, of which waited for: 3 -> 4; matrix products, arithmetic and copies ran while one was open for 1% -> 5% of each run, Pallas kernels for 9% -> 9%
where the time goes in v4:
time: 123 us; the launch traced here: 121 us
  blocking collectives  39.6 us (32%)
  starting transfers between devices  35.8 us (29%)
  Pallas kernels  21 us (17%)
  waiting for transfers between devices  16.6 us (13%)
  local copies, waits for them, and re-layouts  6.79 us (6%)
    all_to_all x1, blocking collectives, exchange(): lax.all_to_all(rows, 'tensor', 0, 0, axis_index_groups=groups, tiled=True)  39.6 us
    all_to_all x2, starting transfers between devices, exchange(): lax.all_to_all(rows, 'tensor', 0, 0, axis_index_groups=groups, tiled=True)  23.2 us
    pallas_call x8, Pallas kernels, run(): inner(*[pltpu.with_memory_space_constraint(arg, pltpu.HBM) if i in any_in...  21 us
    all_to_all x2, waiting for transfers between devices, exchange(): lax.all_to_all(rows, 'tensor', 0, 0, axis_index_groups=groups, tiled=True)  14.8 us
    ppermute x4, starting transfers between devices, shards(): lax.ppermute(head_weight[part * size:(part + 1) * size], 'tensor', partner)  8.65 us
    slice x1, local copies, waits for them, and re-layouts, shards(): head_weight[part * size:(part + 1) * size]  4.35 us
  transfers between devices with their start and end apart: 8, of which 4 were waited for; matrix products, arithmetic and copies ran while one was open for 5% of the time, Pallas kernels for 9%

profile of v4, /device:TPU:6, one launch (start us, length us, event | category | flops | bytes accessed | tf_op | source)
XLA Modules:
  0.0 120.8 jit_solution(6681373639345679047)
XLA Ops:
  0.6 0.0 copy-start
  0.6 0.0 copy-start.1
  0.7 0.7 copy-done.1
  1.4 1.2 gather_hidden.1
  2.6 16.6 %all-to-all-start = ((bf16[64,64,128]{2,1,0:T(8,128)(2,1)}), bf16[64,64,128]{2,1,0:T(8,128)(2,1)S(1)}, u32[]{:S(2)}, u32[]{:S(2)}) async-start(bf16[64,64,128]{2,1,0:T(8,128)(2,1)} %gather_hidden.1), calls=%async_computation | async-start | bytes 2097152 | tf_op jit(solution)/shard_map/gather_hidden/all_to_all | solution.py:336
  19.2 0.2 activations.1
  19.4 0.1 copy.15
  19.5 0.1 reshape.111
  19.6 0.0 copy-done.6
  19.6 0.1 constant_dynamic-slice_fusion
  19.7 0.0 copy-start.7
  19.7 0.0 copy-start.8
  19.7 0.0 copy-start.5
  19.8 0.0 copy-start.2
  19.8 0.0 copy-start.3
  19.8 2.1 %collective-permute-start = (f32[68,128]{1,0:T(8,128)S(1)}, f32[68,128]{1,0:T(8,128)S(1)}, u32[]{:S(2)}, u32[]{:S(2)}) collective-permute-start(f32[68,128]{1,0:T(8,128)S(1)} %pad_maximum_fusion), channel_id=1, source_target_pairs={{0,1},{1,0},{2,3},{3,2},{4,5},{5,4},{6,7},{7,6},{8,9},{9,8},{10,11... | collective-permute-start | bytes 104456 | tf_op jit(solution)/shard_map/activations/ppermute | solution.py:363
  21.8 4.4 %fusion.2 = (bf16[128,4096]{1,0:T(8,128)(2,1)}, bf16[128,4096]{1,0:T(8,128)(2,1)}, bf16[128,4096]{1,0:T(8,128)(2,1)}, bf16[128,4096]{1,0:T(8,128)(2,1)}) fusion(bf16[512,4096]{1,0:T(8,128)(2,1)} %w_own.3), kind=kLoop, calls=%fused_computation.15 | loop fusion | bytes 8388608 | tf_op jit(solution)/shard_map/partner_rows/slice | solution.py:351
  26.2 2.4 %collective-permute-start.1 = (bf16[128,4096]{1,0:T(8,128)(2,1)}, bf16[128,4096]{1,0:T(8,128)(2,1)}, u32[]{:S(2)}, u32[]{:S(2)}) collective-permute-start(bf16[128,4096]{1,0:T(8,128)(2,1)} %get-tuple-element.34), channel_id=1, source_target_pairs={{0,1},{1,0},{2,3},{3,2},{4,5},{5,4},{6,7},{7,6},{8,9},{9,8},{10,11... | collective-permute-start | bytes 3145736 | tf_op jit(solution)/shard_map/partner_rows/ppermute | solution.py:351
  28.6 1.9 %collective-permute-start.2 = (bf16[128,4096]{1,0:T(8,128)(2,1)}, bf16[128,4096]{1,0:T(8,128)(2,1)}, u32[]{:S(2)}, u32[]{:S(2)}) collective-permute-start(bf16[128,4096]{1,0:T(8,128)(2,1)} %get-tuple-element.33), channel_id=1, source_target_pairs={{0,1},{1,0},{2,3},{3,2},{4,5},{5,4},{6,7},{7,6},{8,9},{9,8},{10,11... | collective-permute-start | bytes 3145736 | tf_op jit(solution)/shard_map/partner_rows/ppermute | solution.py:351
  30.5 2.4 %collective-permute-start.3 = (bf16[128,4096]{1,0:T(8,128)(2,1)}, bf16[128,4096]{1,0:T(8,128)(2,1)}, u32[]{:S(2)}, u32[]{:S(2)}) collective-permute-start(bf16[128,4096]{1,0:T(8,128)(2,1)} %get-tuple-element.32), channel_id=1, source_target_pairs={{0,1},{1,0},{2,3},{3,2},{4,5},{5,4},{6,7},{7,6},{8,9},{9,8},{10,11... | collective-permute-start | bytes 3145736 | tf_op jit(solution)/shard_map/partner_rows/ppermute | solution.py:351
  32.9 1.9 %collective-permute-start.4 = (bf16[128,4096]{1,0:T(8,128)(2,1)}, bf16[128,4096]{1,0:T(8,128)(2,1)}, u32[]{:S(2)}, u32[]{:S(2)}) collective-permute-start(bf16[128,4096]{1,0:T(8,128)(2,1)} %get-tuple-element.31), channel_id=1, source_target_pairs={{0,1},{1,0},{2,3},{3,2},{4,5},{5,4},{6,7},{7,6},{8,9},{9,8},{10,11... | collective-permute-start | bytes 3145736 | tf_op jit(solution)/shard_map/partner_rows/ppermute | solution.py:351
  34.9 0.2 stack.9
  35.1 0.1 copy.16
  35.1 0.2 stack.10
  35.3 0.1 copy.17
  35.4 0.1 sub.39
  35.5 0.1 select_n.37
  35.6 0.0 copy-done.5
  35.6 0.1 slice.43.docs
  35.7 0.0 copy-done.3
  35.7 0.4 tables.1.table
  36.1 0.0 collective-permute-done
  36.2 0.0 collective-permute-done.1.refs_0_
  36.2 0.0 collective-permute-done.2.refs_1_
  36.2 0.0 collective-permute-done.3.refs_2_
  36.2 1.6 %collective-permute-done.4.refs_3_ = bf16[128,4096]{1,0:T(8,128)(2,1)} collective-permute-done((bf16[128,4096]{1,0:T(8,128)(2,1)}, bf16[128,4096]{1,0:T(8,128)(2,1)}, u32[]{:S(2)}, u32[]{:S(2)}) %collective-permute-start.4) | collective-permute-done | bytes 1048608 | tf_op jit(solution)/shard_map/partner_rows/ppermute | solution.py:351
  37.8 11.1 %all-to-all-done = bf16[64,64,128]{2,1,0:T(8,128)(2,1)S(1)} async-done(((bf16[64,64,128]{2,1,0:T(8,128)(2,1)}), bf16[64,64,128]{2,1,0:T(8,128)(2,1)S(1)}, u32[]{:S(2)}, u32[]{:S(2)}) %all-to-all-start) | async-done | bytes 1048608 | tf_op jit(solution)/shard_map/gather_hidden/all_to_all | solution.py:336
  48.9 6.8 %scores.1 = (f32[1024,128]{1,0:T(8,128)S(1)}, f32[256,128]{1,0:T(8,128)}) custom-call(bf16[4096,128]{1,0:T(8,128)(2,1)S(1)} %bitcast.18, f32[32,128]{1,0:T(8,128)S(1)} %get-tuple-element.25.gain, f32[64,128]{1,0:T(8,128)S(1)} %slice_add_fusion.acts, bf16[512,4096]{1,0:T(8,128)(2,1)} %w_own.3, bf16[128,4096]{1,0:T(8,128)(2,1)} %collective-permute-done.1.refs_0_, ...), custom_call_target="tpu_custom_call" | custom-call | flops 1073741824 | bytes 10485760 | tf_op jit(solution)/shard_map/scores/pallas_call | solution.py:75
  55.7 6.6 %all-to-all-start.1 = ((f32[64,4,128]{2,1,0:T(4,128)}), f32[64,4,128]{2,1,0:T(4,128)S(1)}, u32[]{:S(2)}, u32[]{:S(2)}) async-start(f32[64,4,128]{2,1,0:T(4,128)} %bitcast.7), calls=%async_computation.1 | async-start | bytes 262144 | tf_op jit(solution)/shard_map/statistics/all_to_all | solution.py:336
  62.3 8.9 %backward.1 = (f32[128,4096]{1,0:T(8,128)}, bf16[128,4096]{1,0:T(8,128)(2,1)}, f32[264,128]{1,0:T(8,128)S(1)}, f32[64,128]{1,0:T(8,128)S(1)}) custom-call(f32[1024,128]{1,0:T(8,128)S(1)} %get-tuple-element.18.logits, s32[1,128]{1,0:T(1,128)S(1)} %and_select_fusion.1.hit, s32[1,1024]{1,0:T(1,128)S(1)} %pad_add_fusion.codes, ...), custom_call_target="tpu_custom_call" | custom-call | flops 3221225472 | bytes 12582912 | tf_op jit(solution)/shard_map/backward/pallas_call | solution.py:75
  71.2 3.7 %all-to-all-done.1 = f32[64,4,128]{2,1,0:T(4,128)S(1)} async-done(((f32[64,4,128]{2,1,0:T(4,128)}), f32[64,4,128]{2,1,0:T(4,128)S(1)}, u32[]{:S(2)}, u32[]{:S(2)}) %all-to-all-start.1) | async-done | bytes 131104 | tf_op jit(solution)/shard_map/statistics/all_to_all | solution.py:336
  74.9 2.2 %scale.1 = bf16[64,72,128]{2,1,0:T(8,128)(2,1)S(1)} custom-call(f32[256,128]{1,0:T(8,128)S(1)} %bitcast.20, f32[128,4096]{1,0:T(8,128)} %get-tuple-element.19.soft_in, bf16[128,4096]{1,0:T(8,128)(2,1)} %get-tuple-element.20.picked_in, f32[264,128]{1,0:T(8,128)S(1)} %get-tuple-element.21.columns), custom_call_target="tpu_custom_call" | custom-call | flops 2000000 | bytes 4194304 | tf_op jit(solution)/shard_map/scale/pallas_call | solution.py:75
  77.1 39.6 %all_to_all.15.blocks = bf16[64,72,128]{2,1,0:T(8,128)(2,1)S(1)} all-to-all(bf16[64,72,128]{2,1,0:T(8,128)(2,1)S(1)} %scale.1), channel_id=1, replica_groups={{0,2,4,6,8,10,12,14,16,18,20,22,24,26,28,30,32,34,36,38,40,42,44,46,48,..., dimensions={0} | all-to-all | bytes 2359296 | tf_op jit(solution)/shard_map/scatter_dnormed/all_to_all | solution.py:336
  116.7 0.4 features.1
  117.2 1.9 %collective-permute-start.5 = (f32[16,32]{1,0:T(8,128)S(1)}, f32[16,32]{1,0:T(8,128)S(1)}, u32[]{:S(2)}, u32[]{:S(2)}) collective-permute-start(f32[16,32]{1,0:T(8,128)S(1)} %get-tuple-element.30), channel_id=1, source_target_pairs={{0,1},{1,0},{2,3},{3,2},{4,5},{5,4},{6,7},{7,6},{8,9},{9,8},{10,11... | collective-permute-start | bytes 6152 | tf_op jit(solution)/shard_map/features/ppermute | solution.py:457
  119.1 1.0 resid_grad.1
  120.1 0.1 collective-permute-done.5
  120.2 0.6 fusion.3
  (19 shorter events, 0.1 us)
Async XLA Ops:
  0.6 18.5 %copy-start = (bf16[2,224,256]{2,1,0:T(8,128)(2,1)S(1)}, bf16[2,224,256]{2,1,0:T(8,128)(2,1)}, u32[]{:S(2)}) copy-start(bf16[2,224,256]{2,1,0:T(8,128)(2,1)} %gate_up.1) | copy-start | bytes 688132
  0.6 0.8 copy-start.1
  1.4 17.8 %copy-start.4 = (s32[224]{0:T(256)S(1)}, s32[224]{0:T(256)}, u32[]{:S(2)}) copy-start(s32[224]{0:T(256)} %param.16) | copy-start | bytes 2692
  1.4 18.2 %copy-start.6 = (s32[512]{0:T(512)S(1)}, s32[512]{0:T(512)}, u32[]{:S(2)}) copy-start(s32[512]{0:T(512)} %param.15) | copy-start | bytes 6148
  2.6 46.4 %all-to-all-start = ((bf16[64,64,128]{2,1,0:T(8,128)(2,1)}), bf16[64,64,128]{2,1,0:T(8,128)(2,1)S(1)}, u32[]{:S(2)}, u32[]{:S(2)}) async-start(bf16[64,64,128]{2,1,0:T(8,128)(2,1)} %gather_hidden.1), calls=%async_computation | async-start | bytes 2097152 | tf_op jit(solution)/shard_map/gather_hidden/all_to_all | solution.py:336
  19.7 15.2 %copy-start.7 = (s32[256]{0:T(256)S(1)}, s32[256]{0:T(256)}, u32[]{:S(2)}) copy-start(s32[256]{0:T(256)} %param.13) | copy-start | bytes 3076
  19.7 15.4 %copy-start.8 = (s32[256]{0:T(256)S(1)}, s32[256]{0:T(256)}, u32[]{:S(2)}) copy-start(s32[256]{0:T(256)} %param.14) | copy-start | bytes 3076
  19.7 15.9 %copy-start.5 = (bf16[4096]{0:T(1024)(128)(2,1)S(1)}, bf16[4096]{0:T(1024)(128)(2,1)}, u32[]{:S(2)}) copy-start(bf16[4096]{0:T(1024)(128)(2,1)} %param.10) | copy-start | bytes 24580
  19.8 15.9 %copy-start.2 = (bf16[2,4096]{1,0:T(2,128)(2,1)S(1)}, bf16[2,4096]{1,0:T(2,128)(2,1)}, u32[]{:S(2)}) copy-start(bf16[2,4096]{1,0:T(2,128)(2,1)} %rows.1) | copy-start | bytes 49156
  19.8 16.0 %copy-start.3 = (s32[2,4096]{1,0:T(2,128)S(1)}, s32[2,4096]{1,0:T(2,128)}, u32[]{:S(2)}) copy-start(s32[2,4096]{1,0:T(2,128)} %codes.1) | copy-start | bytes 98308
  19.8 16.3 %collective-permute-start = (f32[68,128]{1,0:T(8,128)S(1)}, f32[68,128]{1,0:T(8,128)S(1)}, u32[]{:S(2)}, u32[]{:S(2)}) collective-permute-start(f32[68,128]{1,0:T(8,128)S(1)} %pad_maximum_fusion), channel_id=1, source_target_pairs={{0,1},{1,0},{2,3},{3,2},{4,5},{5,4},{6,7},{7,6},{8,9},{9,8},{10,11... | collective-permute-start | bytes 104456 | tf_op jit(solution)/shard_map/activations/ppermute | solution.py:363
  26.2 10.0 %collective-permute-start.1 = (bf16[128,4096]{1,0:T(8,128)(2,1)}, bf16[128,4096]{1,0:T(8,128)(2,1)}, u32[]{:S(2)}, u32[]{:S(2)}) collective-permute-start(bf16[128,4096]{1,0:T(8,128)(2,1)} %get-tuple-element.34), channel_id=1, source_target_pairs={{0,1},{1,0},{2,3},{3,2},{4,5},{5,4},{6,7},{7,6},{8,9},{9,8},{10,11... | collective-permute-start | bytes 3145736 | tf_op jit(solution)/shard_map/partner_rows/ppermute | solution.py:351
  28.6 7.6 %collective-permute-start.2 = (bf16[128,4096]{1,0:T(8,128)(2,1)}, bf16[128,4096]{1,0:T(8,128)(2,1)}, u32[]{:S(2)}, u32[]{:S(2)}) collective-permute-start(bf16[128,4096]{1,0:T(8,128)(2,1)} %get-tuple-element.33), channel_id=1, source_target_pairs={{0,1},{1,0},{2,3},{3,2},{4,5},{5,4},{6,7},{7,6},{8,9},{9,8},{10,11... | collective-permute-start | bytes 3145736 | tf_op jit(solution)/shard_map/partner_rows/ppermute | solution.py:351
  30.5 5.7 %collective-permute-start.3 = (bf16[128,4096]{1,0:T(8,128)(2,1)}, bf16[128,4096]{1,0:T(8,128)(2,1)}, u32[]{:S(2)}, u32[]{:S(2)}) collective-permute-start(bf16[128,4096]{1,0:T(8,128)(2,1)} %get-tuple-element.32), channel_id=1, source_target_pairs={{0,1},{1,0},{2,3},{3,2},{4,5},{5,4},{6,7},{7,6},{8,9},{9,8},{10,11... | collective-permute-start | bytes 3145736 | tf_op jit(solution)/shard_map/partner_rows/ppermute | solution.py:351
  32.9 4.9 %collective-permute-start.4 = (bf16[128,4096]{1,0:T(8,128)(2,1)}, bf16[128,4096]{1,0:T(8,128)(2,1)}, u32[]{:S(2)}, u32[]{:S(2)}) collective-permute-start(bf16[128,4096]{1,0:T(8,128)(2,1)} %get-tuple-element.31), channel_id=1, source_target_pairs={{0,1},{1,0},{2,3},{3,2},{4,5},{5,4},{6,7},{7,6},{8,9},{9,8},{10,11... | collective-permute-start | bytes 3145736 | tf_op jit(solution)/shard_map/partner_rows/ppermute | solution.py:351
  55.7 19.2 %all-to-all-start.1 = ((f32[64,4,128]{2,1,0:T(4,128)}), f32[64,4,128]{2,1,0:T(4,128)S(1)}, u32[]{:S(2)}, u32[]{:S(2)}) async-start(f32[64,4,128]{2,1,0:T(4,128)} %bitcast.7), calls=%async_computation.1 | async-start | bytes 262144 | tf_op jit(solution)/shard_map/statistics/all_to_all | solution.py:336
  117.2 3.1 %collective-permute-start.5 = (f32[16,32]{1,0:T(8,128)S(1)}, f32[16,32]{1,0:T(8,128)S(1)}, u32[]{:S(2)}, u32[]{:S(2)}) collective-permute-start(f32[16,32]{1,0:T(8,128)S(1)} %get-tuple-element.30), channel_id=1, source_target_pairs={{0,1},{1,0},{2,3},{3,2},{4,5},{5,4},{6,7},{7,6},{8,9},{9,8},{10,11... | collective-permute-start | bytes 6152 | tf_op jit(solution)/shard_map/features/ppermute | solution.py:457

commit v5 on v4

--- a/solution.py
+++ b/solution.py
@@ -96,11 +96,13 @@
     out[...] = dot(sign_rows(codes[...]), act, NN)
 
 
-def table_kernel(codes, out):
+def table_kernel(codes, gain, out):
     for block in range(8):
         cols = pl.ds(block * 512, 512)
         out[0:RANK, cols] = sign_rows(codes[0:1, cols])
-        out[RANK : 2 * RANK, cols] = sign_rows(codes[1:2, cols])
+        signs = sign_rows(codes[1:2, cols])
+        out[RANK : 2 * RANK, cols] = signs
+        out[2 * RANK : 3 * RANK, cols] = (signs.astype(f32) * gain[:, cols]).astype(bf16)
 
 
 def norm_pieces(x, gain, xf, hid, normed):
@@ -151,7 +153,7 @@
     return high, (values - high.astype(f32)).astype(bf16)
 
 
-def backward_kernel(logits, hit, codes, table, gain_row, x, gain, w_own, *refs):
+def backward_kernel(logits, hit, codes, table, x, gain, w_own, *refs):
     w_par, refs = refs[:PARTS], refs[PARTS:]
     soft_out, picked_out, columns, aux, xf, hid, normed, w, soft, picked, w_sems, out_sems = refs
     chunks = D // CHUNK
@@ -191,7 +193,7 @@
     left = jnp.concatenate(
         [others.T.astype(bf16), low.astype(f32).T.astype(bf16), onehot.T.astype(bf16)], axis=0
     )
-    sums = jnp.zeros((RANK, 4 * TOK), f32)
+    sums = jnp.zeros((RANK, 3 * TOK), f32)
     outs = []
     for chunk in range(chunks):
         for copy in copies[chunk]:
@@ -212,12 +214,11 @@
             )
             copy.start()
             outs.append(copy)
-        full_high, full_low = split(soft[:, cols] * gain_row[:, cols])
-        pick_high, pick_low = split(pick * gain_row[:, cols])
-        right = jnp.concatenate([full_high, full_low, pick_high, pick_low], axis=0)
-        sums = sums + dot(table[RANK : 2 * RANK, cols], right, NT)
+        full_high, full_low = split(soft[:, cols])
+        right = jnp.concatenate([full_high, full_low, pick.astype(bf16)], axis=0)
+        sums = sums + dot(table[2 * RANK : 3 * RANK, cols], right, NT)
     full_sketch = sums[:, 0:TOK] + sums[:, TOK : 2 * TOK]
-    pick_sketch = sums[:, 2 * TOK : 3 * TOK] + sums[:, 3 * TOK :]
+    pick_sketch = sums[:, 2 * TOK :]
     full_mean = jnp.sum(weights * scores, axis=0, keepdims=True) * (1.0 / D)
     pick_mean = jnp.sum(onehot * scores, axis=0, keepdims=True) * (1.0 / D)
     signs = sign_rows(codes[...])
@@ -366,8 +367,8 @@
         codes = jnp.concatenate([vocab_codes.reshape(1, VOC), codes_par], axis=1)
     with jax.named_scope("tables"):
         table = call(
-            table_kernel, jax.ShapeDtypeStruct((2 * RANK, D), bf16), [], 1, 4000000, 1100000
-        )(model_codes)
+            table_kernel, jax.ShapeDtypeStruct((3 * RANK, D), bf16), [], 2, 4000000, 1600000
+        )(model_codes, gain_row)
         ids = jnp.stack([targets, doc_ids]).reshape(2, PEERS, 2, 2)
         ids = lax.dynamic_index_in_dim(ids, core, axis=2, keepdims=False)
         ids = ids.transpose(0, 2, 1).reshape(2, TOK)
@@ -418,12 +419,12 @@
                 pltpu.SemaphoreType.DMA((D // CHUNK, PARTS + 1)),
                 pltpu.SemaphoreType.DMA((D // CHUNK, 2)),
             ],
-            8 + PARTS,
+            7 + PARTS,
             3 << 30,
             12 * MIB,
-            any_inputs=range(7, 8 + PARTS),
+            any_inputs=range(6, 7 + PARTS),
             any_outs=(0, 1),
-        )(logits, hit, codes, table, gain_row, gathered, gain_blk, head_weight, *w_par)
+        )(logits, hit, codes, table, gathered, gain_blk, head_weight, *w_par)
     with jax.named_scope("scale"):
         blocks = call(
             scale_kernel,

time: 123 us -> 122 us (level)
  transfers between devices with their start and end apart: 8 -> 8, of which waited for: 4 -> 4; matrix products, arithmetic and copies ran while one was open for 5% -> 5% of each run, Pallas kernels for 9% -> 8%
where the time goes in v5:
time: 122 us; the launch traced here: 120 us
  blocking collectives  38.4 us (31%)
  starting transfers between devices  35.8 us (29%)
  Pallas kernels  20 us (16%)
  waiting for transfers between devices  17.7 us (15%)
  local copies, waits for them, and re-layouts  6.79 us (6%)
    all_to_all x1, blocking collectives, exchange(): lax.all_to_all(rows, 'tensor', 0, 0, axis_index_groups=groups, tiled=True)  38.4 us
    all_to_all x2, starting transfers between devices, exchange(): lax.all_to_all(rows, 'tensor', 0, 0, axis_index_groups=groups, tiled=True)  23.2 us
    pallas_call x8, Pallas kernels, run(): inner(*[pltpu.with_memory_space_constraint(arg, pltpu.HBM) if i in any_in...  20 us
    all_to_all x2, waiting for transfers between devices, exchange(): lax.all_to_all(rows, 'tensor', 0, 0, axis_index_groups=groups, tiled=True)  16 us
    ppermute x4, starting transfers between devices, shards(): lax.ppermute(head_weight[part * size:(part + 1) * size], 'tensor', partner)  8.65 us
    slice x1, local copies, waits for them, and re-layouts, shards(): head_weight[part * size:(part + 1) * size]  4.35 us
  transfers between devices with their start and end apart: 8, of which 4 were waited for; matrix products, arithmetic and copies ran while one was open for 5% of the time, Pallas kernels for 8%

profile of v5, /device:TPU:6, one launch (start us, length us, event | category | flops | bytes accessed | tf_op | source)
XLA Modules:
  0.0 119.7 jit_solution(13042340043446925243)
XLA Ops:
  0.6 0.0 copy-start
  0.6 0.0 copy-start.1
  0.7 0.7 copy-done.1
  1.4 1.2 gather_hidden.1
  2.6 16.6 %all-to-all-start = ((bf16[64,64,128]{2,1,0:T(8,128)(2,1)}), bf16[64,64,128]{2,1,0:T(8,128)(2,1)S(1)}, u32[]{:S(2)}, u32[]{:S(2)}) async-start(bf16[64,64,128]{2,1,0:T(8,128)(2,1)} %gather_hidden.1), calls=%async_computation | async-start | bytes 2097152 | tf_op jit(solution)/shard_map/gather_hidden/all_to_all | solution.py:337
  19.2 0.0 copy-done
  19.2 0.0 copy-done.4
  19.2 0.2 activations.1
  19.4 0.1 copy.15
  19.5 0.1 reshape.111
  19.6 0.1 constant_dynamic-slice_fusion
  19.7 0.0 copy-start.7
  19.7 0.0 copy-start.8
  19.7 0.0 copy-start.5
  19.8 0.0 copy-start.2
  19.8 0.0 copy-start.3
  19.8 2.1 %collective-permute-start = (f32[68,128]{1,0:T(8,128)S(1)}, f32[68,128]{1,0:T(8,128)S(1)}, u32[]{:S(2)}, u32[]{:S(2)}) collective-permute-start(f32[68,128]{1,0:T(8,128)S(1)} %pad_maximum_fusion), channel_id=1, source_target_pairs={{0,1},{1,0},{2,3},{3,2},{4,5},{5,4},{6,7},{7,6},{8,9},{9,8},{10,11... | collective-permute-start | bytes 104456 | tf_op jit(solution)/shard_map/activations/ppermute | solution.py:364
  21.8 4.4 %fusion.2 = (bf16[128,4096]{1,0:T(8,128)(2,1)}, bf16[128,4096]{1,0:T(8,128)(2,1)}, bf16[128,4096]{1,0:T(8,128)(2,1)}, bf16[128,4096]{1,0:T(8,128)(2,1)}) fusion(bf16[512,4096]{1,0:T(8,128)(2,1)} %w_own.3), kind=kLoop, calls=%fused_computation.15 | loop fusion | bytes 8388608 | tf_op jit(solution)/shard_map/partner_rows/slice | solution.py:352
  26.2 2.4 %collective-permute-start.1 = (bf16[128,4096]{1,0:T(8,128)(2,1)}, bf16[128,4096]{1,0:T(8,128)(2,1)}, u32[]{:S(2)}, u32[]{:S(2)}) collective-permute-start(bf16[128,4096]{1,0:T(8,128)(2,1)} %get-tuple-element.34), channel_id=1, source_target_pairs={{0,1},{1,0},{2,3},{3,2},{4,5},{5,4},{6,7},{7,6},{8,9},{9,8},{10,11... | collective-permute-start | bytes 3145736 | tf_op jit(solution)/shard_map/partner_rows/ppermute | solution.py:352
  28.6 1.9 %collective-permute-start.2 = (bf16[128,4096]{1,0:T(8,128)(2,1)}, bf16[128,4096]{1,0:T(8,128)(2,1)}, u32[]{:S(2)}, u32[]{:S(2)}) collective-permute-start(bf16[128,4096]{1,0:T(8,128)(2,1)} %get-tuple-element.33), channel_id=1, source_target_pairs={{0,1},{1,0},{2,3},{3,2},{4,5},{5,4},{6,7},{7,6},{8,9},{9,8},{10,11... | collective-permute-start | bytes 3145736 | tf_op jit(solution)/shard_map/partner_rows/ppermute | solution.py:352
  30.5 2.4 %collective-permute-start.3 = (bf16[128,4096]{1,0:T(8,128)(2,1)}, bf16[128,4096]{1,0:T(8,128)(2,1)}, u32[]{:S(2)}, u32[]{:S(2)}) collective-permute-start(bf16[128,4096]{1,0:T(8,128)(2,1)} %get-tuple-element.32), channel_id=1, source_target_pairs={{0,1},{1,0},{2,3},{3,2},{4,5},{5,4},{6,7},{7,6},{8,9},{9,8},{10,11... | collective-permute-start | bytes 3145736 | tf_op jit(solution)/shard_map/partner_rows/ppermute | solution.py:352
  32.9 1.9 %collective-permute-start.4 = (bf16[128,4096]{1,0:T(8,128)(2,1)}, bf16[128,4096]{1,0:T(8,128)(2,1)}, u32[]{:S(2)}, u32[]{:S(2)}) collective-permute-start(bf16[128,4096]{1,0:T(8,128)(2,1)} %get-tuple-element.31), channel_id=1, source_target_pairs={{0,1},{1,0},{2,3},{3,2},{4,5},{5,4},{6,7},{7,6},{8,9},{9,8},{10,11... | collective-permute-start | bytes 3145736 | tf_op jit(solution)/shard_map/partner_rows/ppermute | solution.py:352
  34.9 0.0 copy-done.7
  34.9 0.2 stack.9
  35.1 0.1 copy.16
  35.1 0.2 stack.10
  35.3 0.1 copy.17
  35.4 0.1 sub.39
  35.5 0.1 select_n.37
  35.6 0.1 slice.43.docs
  35.7 0.5 tables.1.table
  36.2 0.0 collective-permute-done
  36.3 0.0 collective-permute-done.1.refs_0_
  36.3 0.0 collective-permute-done.2.refs_1_
  36.3 0.0 collective-permute-done.3.refs_2_
  36.3 1.5 %collective-permute-done.4.refs_3_ = bf16[128,4096]{1,0:T(8,128)(2,1)} collective-permute-done((bf16[128,4096]{1,0:T(8,128)(2,1)}, bf16[128,4096]{1,0:T(8,128)(2,1)}, u32[]{:S(2)}, u32[]{:S(2)}) %collective-permute-start.4) | collective-permute-done | bytes 1048608 | tf_op jit(solution)/shard_map/partner_rows/ppermute | solution.py:352
  37.8 11.1 %all-to-all-done = bf16[64,64,128]{2,1,0:T(8,128)(2,1)S(1)} async-done(((bf16[64,64,128]{2,1,0:T(8,128)(2,1)}), bf16[64,64,128]{2,1,0:T(8,128)(2,1)S(1)}, u32[]{:S(2)}, u32[]{:S(2)}) %all-to-all-start) | async-done | bytes 1048608 | tf_op jit(solution)/shard_map/gather_hidden/all_to_all | solution.py:337
  48.9 6.8 %scores.1 = (f32[1024,128]{1,0:T(8,128)S(1)}, f32[256,128]{1,0:T(8,128)}) custom-call(bf16[4096,128]{1,0:T(8,128)(2,1)S(1)} %bitcast.18, f32[32,128]{1,0:T(8,128)S(1)} %get-tuple-element.25.gain, f32[64,128]{1,0:T(8,128)S(1)} %slice_add_fusion.acts, bf16[512,4096]{1,0:T(8,128)(2,1)} %w_own.3, bf16[128,4096]{1,0:T(8,128)(2,1)} %collective-permute-done.1.refs_0_, ...), custom_call_target="tpu_custom_call" | custom-call | flops 1073741824 | bytes 10485760 | tf_op jit(solution)/shard_map/scores/pallas_call | solution.py:75
  55.7 6.6 %all-to-all-start.1 = ((f32[64,4,128]{2,1,0:T(4,128)}), f32[64,4,128]{2,1,0:T(4,128)S(1)}, u32[]{:S(2)}, u32[]{:S(2)}) async-start(f32[64,4,128]{2,1,0:T(4,128)} %bitcast.7), calls=%async_computation.1 | async-start | bytes 262144 | tf_op jit(solution)/shard_map/statistics/all_to_all | solution.py:337
  62.3 7.7 %backward.1 = (f32[128,4096]{1,0:T(8,128)}, bf16[128,4096]{1,0:T(8,128)(2,1)}, f32[264,128]{1,0:T(8,128)S(1)}, f32[64,128]{1,0:T(8,128)S(1)}) custom-call(f32[1024,128]{1,0:T(8,128)S(1)} %get-tuple-element.18.logits, s32[1,128]{1,0:T(1,128)S(1)} %and_select_fusion.1.hit, s32[1,1024]{1,0:T(1,128)S(1)} %pad_add_fusion.codes, ...), custom_call_target="tpu_custom_call" | custom-call | flops 3221225472 | bytes 12582912 | tf_op jit(solution)/shard_map/backward/pallas_call | solution.py:75
  70.0 4.9 %all-to-all-done.1 = f32[64,4,128]{2,1,0:T(4,128)S(1)} async-done(((f32[64,4,128]{2,1,0:T(4,128)}), f32[64,4,128]{2,1,0:T(4,128)S(1)}, u32[]{:S(2)}, u32[]{:S(2)}) %all-to-all-start.1) | async-done | bytes 131104 | tf_op jit(solution)/shard_map/statistics/all_to_all | solution.py:337
  74.9 2.2 %scale.1 = bf16[64,72,128]{2,1,0:T(8,128)(2,1)S(1)} custom-call(f32[256,128]{1,0:T(8,128)S(1)} %bitcast.20, f32[128,4096]{1,0:T(8,128)} %get-tuple-element.19.soft_in, bf16[128,4096]{1,0:T(8,128)(2,1)} %get-tuple-element.20.picked_in, f32[264,128]{1,0:T(8,128)S(1)} %get-tuple-element.21.columns), custom_call_target="tpu_custom_call" | custom-call | flops 2000000 | bytes 4194304 | tf_op jit(solution)/shard_map/scale/pallas_call | solution.py:75
  77.1 38.4 %all_to_all.15.blocks = bf16[64,72,128]{2,1,0:T(8,128)(2,1)S(1)} all-to-all(bf16[64,72,128]{2,1,0:T(8,128)(2,1)S(1)} %scale.1), channel_id=1, replica_groups={{0,2,4,6,8,10,12,14,16,18,20,22,24,26,28,30,32,34,36,38,40,42,44,46,48,..., dimensions={0} | all-to-all | bytes 2359296 | tf_op jit(solution)/shard_map/scatter_dnormed/all_to_all | solution.py:337
  115.6 0.4 features.1
  116.0 1.9 %collective-permute-start.5 = (f32[16,32]{1,0:T(8,128)S(1)}, f32[16,32]{1,0:T(8,128)S(1)}, u32[]{:S(2)}, u32[]{:S(2)}) collective-permute-start(f32[16,32]{1,0:T(8,128)S(1)} %get-tuple-element.30), channel_id=1, source_target_pairs={{0,1},{1,0},{2,3},{3,2},{4,5},{5,4},{6,7},{7,6},{8,9},{9,8},{10,11... | collective-permute-start | bytes 6152 | tf_op jit(solution)/shard_map/features/ppermute | solution.py:458
  117.9 1.0 resid_grad.1
  118.9 0.1 collective-permute-done.5
  119.1 0.6 fusion.3
  (19 shorter events, 0.1 us)
Async XLA Ops:
  0.6 18.5 %copy-start = (bf16[2,224,256]{2,1,0:T(8,128)(2,1)S(1)}, bf16[2,224,256]{2,1,0:T(8,128)(2,1)}, u32[]{:S(2)}) copy-start(bf16[2,224,256]{2,1,0:T(8,128)(2,1)} %gate_up.1) | copy-start | bytes 688132
  0.6 0.8 copy-start.1
  1.4 17.8 %copy-start.4 = (s32[224]{0:T(256)S(1)}, s32[224]{0:T(256)}, u32[]{:S(2)}) copy-start(s32[224]{0:T(256)} %param.16) | copy-start | bytes 2692
  1.4 18.2 %copy-start.6 = (s32[512]{0:T(512)S(1)}, s32[512]{0:T(512)}, u32[]{:S(2)}) copy-start(s32[512]{0:T(512)} %param.15) | copy-start | bytes 6148
  2.6 46.4 %all-to-all-start = ((bf16[64,64,128]{2,1,0:T(8,128)(2,1)}), bf16[64,64,128]{2,1,0:T(8,128)(2,1)S(1)}, u32[]{:S(2)}, u32[]{:S(2)}) async-start(bf16[64,64,128]{2,1,0:T(8,128)(2,1)} %gather_hidden.1), calls=%async_computation | async-start | bytes 2097152 | tf_op jit(solution)/shard_map/gather_hidden/all_to_all | solution.py:337
  19.7 15.2 %copy-start.7 = (s32[256]{0:T(256)S(1)}, s32[256]{0:T(256)}, u32[]{:S(2)}) copy-start(s32[256]{0:T(256)} %param.13) | copy-start | bytes 3076
  19.7 15.4 %copy-start.8 = (s32[256]{0:T(256)S(1)}, s32[256]{0:T(256)}, u32[]{:S(2)}) copy-start(s32[256]{0:T(256)} %param.14) | copy-start | bytes 3076
  19.7 15.9 %copy-start.5 = (bf16[4096]{0:T(1024)(128)(2,1)S(1)}, bf16[4096]{0:T(1024)(128)(2,1)}, u32[]{:S(2)}) copy-start(bf16[4096]{0:T(1024)(128)(2,1)} %param.10) | copy-start | bytes 24580
  19.8 15.9 %copy-start.2 = (bf16[2,4096]{1,0:T(2,128)(2,1)S(1)}, bf16[2,4096]{1,0:T(2,128)(2,1)}, u32[]{:S(2)}) copy-start(bf16[2,4096]{1,0:T(2,128)(2,1)} %rows.1) | copy-start | bytes 49156
  19.8 16.0 %copy-start.3 = (s32[2,4096]{1,0:T(2,128)S(1)}, s32[2,4096]{1,0:T(2,128)}, u32[]{:S(2)}) copy-start(s32[2,4096]{1,0:T(2,128)} %codes.1) | copy-start | bytes 98308
  19.8 16.4 %collective-permute-start = (f32[68,128]{1,0:T(8,128)S(1)}, f32[68,128]{1,0:T(8,128)S(1)}, u32[]{:S(2)}, u32[]{:S(2)}) collective-permute-start(f32[68,128]{1,0:T(8,128)S(1)} %pad_maximum_fusion), channel_id=1, source_target_pairs={{0,1},{1,0},{2,3},{3,2},{4,5},{5,4},{6,7},{7,6},{8,9},{9,8},{10,11... | collective-permute-start | bytes 104456 | tf_op jit(solution)/shard_map/activations/ppermute | solution.py:364
  26.2 10.1 %collective-permute-start.1 = (bf16[128,4096]{1,0:T(8,128)(2,1)}, bf16[128,4096]{1,0:T(8,128)(2,1)}, u32[]{:S(2)}, u32[]{:S(2)}) collective-permute-start(bf16[128,4096]{1,0:T(8,128)(2,1)} %get-tuple-element.34), channel_id=1, source_target_pairs={{0,1},{1,0},{2,3},{3,2},{4,5},{5,4},{6,7},{7,6},{8,9},{9,8},{10,11... | collective-permute-start | bytes 3145736 | tf_op jit(solution)/shard_map/partner_rows/ppermute | solution.py:352
  28.6 7.7 %collective-permute-start.2 = (bf16[128,4096]{1,0:T(8,128)(2,1)}, bf16[128,4096]{1,0:T(8,128)(2,1)}, u32[]{:S(2)}, u32[]{:S(2)}) collective-permute-start(bf16[128,4096]{1,0:T(8,128)(2,1)} %get-tuple-element.33), channel_id=1, source_target_pairs={{0,1},{1,0},{2,3},{3,2},{4,5},{5,4},{6,7},{7,6},{8,9},{9,8},{10,11... | collective-permute-start | bytes 3145736 | tf_op jit(solution)/shard_map/partner_rows/ppermute | solution.py:352
  30.5 5.8 %collective-permute-start.3 = (bf16[128,4096]{1,0:T(8,128)(2,1)}, bf16[128,4096]{1,0:T(8,128)(2,1)}, u32[]{:S(2)}, u32[]{:S(2)}) collective-permute-start(bf16[128,4096]{1,0:T(8,128)(2,1)} %get-tuple-element.32), channel_id=1, source_target_pairs={{0,1},{1,0},{2,3},{3,2},{4,5},{5,4},{6,7},{7,6},{8,9},{9,8},{10,11... | collective-permute-start | bytes 3145736 | tf_op jit(solution)/shard_map/partner_rows/ppermute | solution.py:352
  32.9 4.9 %collective-permute-start.4 = (bf16[128,4096]{1,0:T(8,128)(2,1)}, bf16[128,4096]{1,0:T(8,128)(2,1)}, u32[]{:S(2)}, u32[]{:S(2)}) collective-permute-start(bf16[128,4096]{1,0:T(8,128)(2,1)} %get-tuple-element.31), channel_id=1, source_target_pairs={{0,1},{1,0},{2,3},{3,2},{4,5},{5,4},{6,7},{7,6},{8,9},{9,8},{10,11... | collective-permute-start | bytes 3145736 | tf_op jit(solution)/shard_map/partner_rows/ppermute | solution.py:352
  55.7 19.2 %all-to-all-start.1 = ((f32[64,4,128]{2,1,0:T(4,128)}), f32[64,4,128]{2,1,0:T(4,128)S(1)}, u32[]{:S(2)}, u32[]{:S(2)}) async-start(f32[64,4,128]{2,1,0:T(4,128)} %bitcast.7), calls=%async_computation.1 | async-start | bytes 262144 | tf_op jit(solution)/shard_map/statistics/all_to_all | solution.py:337
  116.0 3.1 %collective-permute-start.5 = (f32[16,32]{1,0:T(8,128)S(1)}, f32[16,32]{1,0:T(8,128)S(1)}, u32[]{:S(2)}, u32[]{:S(2)}) collective-permute-start(f32[16,32]{1,0:T(8,128)S(1)} %get-tuple-element.30), channel_id=1, source_target_pairs={{0,1},{1,0},{2,3},{3,2},{4,5},{5,4},{6,7},{7,6},{8,9},{9,8},{10,11... | collective-permute-start | bytes 6152 | tf_op jit(solution)/shard_map/features/ppermute | solution.py:458

commit v6 on v5

--- a/solution.py
+++ b/solution.py
@@ -188,7 +188,6 @@
     weights = jnp.exp(scores - top)
     others = jnp.where(chosen, 0.0, weights)
     at_target = jnp.sum(jnp.where(chosen, weights, 0.0), axis=0, keepdims=True)
-    at_target_rows = jnp.broadcast_to(at_target, (LANES, LANES)).T
     high, low = split(others)
     left = jnp.concatenate(
         [others.T.astype(bf16), low.astype(f32).T.astype(bf16), onehot.T.astype(bf16)], axis=0
@@ -202,10 +201,7 @@
         both = dot(left, w[:, cols], NN)
         pick = both[2 * TOK :, :]
         full = both[0:TOK, :] + both[TOK : 2 * TOK, :]
-        for k in range(CHUNK // LANES):
-            lanes = slice(k * LANES, (k + 1) * LANES)
-            place = slice(chunk * CHUNK + k * LANES, chunk * CHUNK + (k + 1) * LANES)
-            soft[:, place] = full[:, lanes] + at_target_rows * pick[:, lanes]
+        soft[:, cols] = full
         picked[:, cols] = pick.astype(bf16)
         spot = pl.ds(chunk * CHUNK, CHUNK)
         for sem, (source, target) in enumerate(((soft, soft_out), (picked, picked_out))):
@@ -214,21 +210,22 @@
             )
             copy.start()
             outs.append(copy)
-        full_high, full_low = split(soft[:, cols])
+        full_high, full_low = split(full)
         right = jnp.concatenate([full_high, full_low, pick.astype(bf16)], axis=0)
         sums = sums + dot(table[2 * RANK : 3 * RANK, cols], right, NT)
     full_sketch = sums[:, 0:TOK] + sums[:, TOK : 2 * TOK]
     pick_sketch = sums[:, 2 * TOK :]
-    full_mean = jnp.sum(weights * scores, axis=0, keepdims=True) * (1.0 / D)
+    full_mean = jnp.sum(others * scores, axis=0, keepdims=True) * (1.0 / D)
     pick_mean = jnp.sum(onehot * scores, axis=0, keepdims=True) * (1.0 / D)
     signs = sign_rows(codes[...])
     pick_vocab = dot(signs, onehot.astype(bf16), NN)
-    soft_vocab = dot(signs, high, NN) + dot(signs, low, NN) + at_target * pick_vocab
+    soft_vocab = dot(signs, high, NN) + dot(signs, low, NN)
     columns[0:RANK, :] = soft_vocab
     columns[RANK : 2 * RANK, :] = pick_vocab
     columns[2 * RANK : 3 * RANK, :] = inv * (full_sketch - unit_sketch * full_mean)
     columns[3 * RANK : 4 * RANK, :] = inv * (pick_sketch - unit_sketch * pick_mean)
     columns[4 * RANK : 4 * RANK + 8, :] = jnp.broadcast_to(top, (8, LANES))
+    columns[4 * RANK + 8 : 4 * RANK + 16, :] = jnp.broadcast_to(at_target, (8, LANES))
     for copy in outs:
         copy.wait()
 
@@ -249,18 +246,20 @@
     top = jnp.max(tops, axis=0, keepdims=True)
     denominator = jnp.sum(totals * jnp.exp(tops - top), axis=0, keepdims=True)
     scale = jnp.exp(columns[4 * RANK : 4 * RANK + 1, :] - top) / denominator
+    target = scale * columns[4 * RANK + 8 : 4 * RANK + 9, :] - 1.0
     scale_rows = jnp.broadcast_to(scale, (LANES, LANES)).T
+    target_rows = jnp.broadcast_to(target, (LANES, LANES)).T
     for k in range(PIECES):
         if k % (CHUNK // LANES) == 0:
             chunk = k // (CHUNK // LANES)
             copies[2 * chunk].wait()
             copies[2 * chunk + 1].wait()
         lanes = slice(k * LANES, (k + 1) * LANES)
-        piece = scale_rows * soft[:, lanes] - picked[:, lanes].astype(f32)
+        piece = scale_rows * soft[:, lanes] + target_rows * picked[:, lanes].astype(f32)
         df[pl.ds(k, PEERS, stride=PITCH), :] = piece[0:PEERS, :]
         df[pl.ds(PIECES + k, PEERS, stride=PITCH), :] = piece[PEERS:TOK, :]
-    vocab_sketch = scale * columns[0:RANK, :] - columns[RANK : 2 * RANK, :]
-    grad_sketch = scale * columns[2 * RANK : 3 * RANK, :] - columns[3 * RANK : 4 * RANK, :]
+    vocab_sketch = scale * columns[0:RANK, :] + target * columns[RANK : 2 * RANK, :]
+    grad_sketch = scale * columns[2 * RANK : 3 * RANK, :] + target * columns[3 * RANK : 4 * RANK, :]
     acts = jnp.broadcast_to(acts, (PEERS, LANES))
     for place, values in enumerate((vocab_sketch, grad_sketch, acts)):
         high = values.astype(bf16).astype(f32)
@@ -408,7 +407,7 @@
             (
                 jax.ShapeDtypeStruct((TOK, D), f32),
                 jax.ShapeDtypeStruct((TOK, D), bf16),
-                jax.ShapeDtypeStruct((4 * RANK + 8, LANES), f32),
+                jax.ShapeDtypeStruct((4 * RANK + 16, LANES), f32),
                 jax.ShapeDtypeStruct((RANK, LANES), f32),
             ),
             norm_scratch

time: 122 us -> 122 us (level)
  no operation moved by 1% of the time
where the time goes in v6:
time: 122 us; the launch traced here: 120 us
  blocking collectives  38.9 us (32%)
  starting transfers between devices  35.8 us (29%)
  Pallas kernels  20.5 us (17%)
  waiting for transfers between devices  17.2 us (14%)
  local copies, waits for them, and re-layouts  6.79 us (6%)
    all_to_all x1, blocking collectives, exchange(): lax.all_to_all(rows, 'tensor', 0, 0, axis_index_groups=groups, tiled=True)  38.9 us
    all_to_all x2, starting transfers between devices, exchange(): lax.all_to_all(rows, 'tensor', 0, 0, axis_index_groups=groups, tiled=True)  23.2 us
    pallas_call x8, Pallas kernels, run(): inner(*[pltpu.with_memory_space_constraint(arg, pltpu.HBM) if i in any_in...  20.5 us
    all_to_all x2, waiting for transfers between devices, exchange(): lax.all_to_all(rows, 'tensor', 0, 0, axis_index_groups=groups, tiled=True)  15.5 us
    ppermute x4, starting transfers between devices, shards(): lax.ppermute(head_weight[part * size:(part + 1) * size], 'tensor', partner)  8.65 us
    slice x1, local copies, waits for them, and re-layouts, shards(): head_weight[part * size:(part + 1) * size]  4.35 us
  transfers between devices with their start and end apart: 8, of which 4 were waited for; matrix products, arithmetic and copies ran while one was open for 5% of the time, Pallas kernels for 8%

profile of v6, /device:TPU:6, one launch (start us, length us, event | category | flops | bytes accessed | tf_op | source)
XLA Modules:
  0.0 120.2 jit_solution(5343087652102261765)
XLA Ops:
  0.6 0.0 copy-start
  0.6 0.0 copy-start.1
  0.7 0.7 copy-done.1
  1.4 1.2 gather_hidden.1
  2.6 16.6 %all-to-all-start = ((bf16[64,64,128]{2,1,0:T(8,128)(2,1)}), bf16[64,64,128]{2,1,0:T(8,128)(2,1)S(1)}, u32[]{:S(2)}, u32[]{:S(2)}) async-start(bf16[64,64,128]{2,1,0:T(8,128)(2,1)} %gather_hidden.1), calls=%async_computation | async-start | bytes 2097152 | tf_op jit(solution)/shard_map/gather_hidden/all_to_all | solution.py:336
  19.2 0.2 activations.1
  19.4 0.1 copy.15
  19.5 0.1 reshape.111
  19.6 0.0 copy-done.6
  19.6 0.1 constant_dynamic-slice_fusion
  19.7 0.0 copy-start.7
  19.7 0.0 copy-start.8
  19.7 0.0 copy-start.5
  19.8 0.0 copy-start.2
  19.8 0.0 copy-start.3
  19.8 2.1 %collective-permute-start = (f32[68,128]{1,0:T(8,128)S(1)}, f32[68,128]{1,0:T(8,128)S(1)}, u32[]{:S(2)}, u32[]{:S(2)}) collective-permute-start(f32[68,128]{1,0:T(8,128)S(1)} %pad_maximum_fusion), channel_id=1, source_target_pairs={{0,1},{1,0},{2,3},{3,2},{4,5},{5,4},{6,7},{7,6},{8,9},{9,8},{10,11... | collective-permute-start | bytes 104456 | tf_op jit(solution)/shard_map/activations/ppermute | solution.py:363
  21.8 4.4 %fusion.2 = (bf16[128,4096]{1,0:T(8,128)(2,1)}, bf16[128,4096]{1,0:T(8,128)(2,1)}, bf16[128,4096]{1,0:T(8,128)(2,1)}, bf16[128,4096]{1,0:T(8,128)(2,1)}) fusion(bf16[512,4096]{1,0:T(8,128)(2,1)} %w_own.3), kind=kLoop, calls=%fused_computation.15 | loop fusion | bytes 8388608 | tf_op jit(solution)/shard_map/partner_rows/slice | solution.py:351
  26.2 2.4 %collective-permute-start.1 = (bf16[128,4096]{1,0:T(8,128)(2,1)}, bf16[128,4096]{1,0:T(8,128)(2,1)}, u32[]{:S(2)}, u32[]{:S(2)}) collective-permute-start(bf16[128,4096]{1,0:T(8,128)(2,1)} %get-tuple-element.34), channel_id=1, source_target_pairs={{0,1},{1,0},{2,3},{3,2},{4,5},{5,4},{6,7},{7,6},{8,9},{9,8},{10,11... | collective-permute-start | bytes 3145736 | tf_op jit(solution)/shard_map/partner_rows/ppermute | solution.py:351
  28.6 1.9 %collective-permute-start.2 = (bf16[128,4096]{1,0:T(8,128)(2,1)}, bf16[128,4096]{1,0:T(8,128)(2,1)}, u32[]{:S(2)}, u32[]{:S(2)}) collective-permute-start(bf16[128,4096]{1,0:T(8,128)(2,1)} %get-tuple-element.33), channel_id=1, source_target_pairs={{0,1},{1,0},{2,3},{3,2},{4,5},{5,4},{6,7},{7,6},{8,9},{9,8},{10,11... | collective-permute-start | bytes 3145736 | tf_op jit(solution)/shard_map/partner_rows/ppermute | solution.py:351
  30.5 2.4 %collective-permute-start.3 = (bf16[128,4096]{1,0:T(8,128)(2,1)}, bf16[128,4096]{1,0:T(8,128)(2,1)}, u32[]{:S(2)}, u32[]{:S(2)}) collective-permute-start(bf16[128,4096]{1,0:T(8,128)(2,1)} %get-tuple-element.32), channel_id=1, source_target_pairs={{0,1},{1,0},{2,3},{3,2},{4,5},{5,4},{6,7},{7,6},{8,9},{9,8},{10,11... | collective-permute-start | bytes 3145736 | tf_op jit(solution)/shard_map/partner_rows/ppermute | solution.py:351
  32.9 1.9 %collective-permute-start.4 = (bf16[128,4096]{1,0:T(8,128)(2,1)}, bf16[128,4096]{1,0:T(8,128)(2,1)}, u32[]{:S(2)}, u32[]{:S(2)}) collective-permute-start(bf16[128,4096]{1,0:T(8,128)(2,1)} %get-tuple-element.31), channel_id=1, source_target_pairs={{0,1},{1,0},{2,3},{3,2},{4,5},{5,4},{6,7},{7,6},{8,9},{9,8},{10,11... | collective-permute-start | bytes 3145736 | tf_op jit(solution)/shard_map/partner_rows/ppermute | solution.py:351
  34.9 0.2 stack.9
  35.1 0.1 copy.16
  35.1 0.2 stack.10
  35.3 0.1 copy.17
  35.4 0.1 sub.39
  35.5 0.1 select_n.37
  35.6 0.0 copy-done.5
  35.6 0.1 slice.43.docs
  35.7 0.0 copy-done.3
  35.7 0.5 tables.1.table
  36.2 0.0 collective-permute-done
  36.3 0.0 collective-permute-done.1.refs_0_
  36.3 0.0 collective-permute-done.2.refs_1_
  36.3 0.0 collective-permute-done.3.refs_2_
  36.3 1.5 %collective-permute-done.4.refs_3_ = bf16[128,4096]{1,0:T(8,128)(2,1)} collective-permute-done((bf16[128,4096]{1,0:T(8,128)(2,1)}, bf16[128,4096]{1,0:T(8,128)(2,1)}, u32[]{:S(2)}, u32[]{:S(2)}) %collective-permute-start.4) | collective-permute-done | bytes 1048608 | tf_op jit(solution)/shard_map/partner_rows/ppermute | solution.py:351
  37.8 11.1 %all-to-all-done = bf16[64,64,128]{2,1,0:T(8,128)(2,1)S(1)} async-done(((bf16[64,64,128]{2,1,0:T(8,128)(2,1)}), bf16[64,64,128]{2,1,0:T(8,128)(2,1)S(1)}, u32[]{:S(2)}, u32[]{:S(2)}) %all-to-all-start) | async-done | bytes 1048608 | tf_op jit(solution)/shard_map/gather_hidden/all_to_all | solution.py:336
  48.9 6.8 %scores.1 = (f32[1024,128]{1,0:T(8,128)S(1)}, f32[256,128]{1,0:T(8,128)}) custom-call(bf16[4096,128]{1,0:T(8,128)(2,1)S(1)} %bitcast.18, f32[32,128]{1,0:T(8,128)S(1)} %get-tuple-element.25.gain, f32[64,128]{1,0:T(8,128)S(1)} %slice_add_fusion.acts, bf16[512,4096]{1,0:T(8,128)(2,1)} %w_own.3, bf16[128,4096]{1,0:T(8,128)(2,1)} %collective-permute-done.1.refs_0_, ...), custom_call_target="tpu_custom_call" | custom-call | flops 1073741824 | bytes 10485760 | tf_op jit(solution)/shard_map/scores/pallas_call | solution.py:75
  55.7 6.6 %all-to-all-start.1 = ((f32[64,4,128]{2,1,0:T(4,128)}), f32[64,4,128]{2,1,0:T(4,128)S(1)}, u32[]{:S(2)}, u32[]{:S(2)}) async-start(f32[64,4,128]{2,1,0:T(4,128)} %bitcast.7), calls=%async_computation.1 | async-start | bytes 262144 | tf_op jit(solution)/shard_map/statistics/all_to_all | solution.py:336
  62.3 8.2 %backward.1 = (f32[128,4096]{1,0:T(8,128)}, bf16[128,4096]{1,0:T(8,128)(2,1)}, f32[272,128]{1,0:T(8,128)S(1)}, f32[64,128]{1,0:T(8,128)S(1)}) custom-call(f32[1024,128]{1,0:T(8,128)S(1)} %get-tuple-element.18.logits, s32[1,128]{1,0:T(1,128)S(1)} %and_select_fusion.1.hit, s32[1,1024]{1,0:T(1,128)S(1)} %pad_add_fusion.codes, ...), custom_call_target="tpu_custom_call" | custom-call | flops 3221225472 | bytes 12582912 | tf_op jit(solution)/shard_map/backward/pallas_call | solution.py:75
  70.5 4.4 %all-to-all-done.1 = f32[64,4,128]{2,1,0:T(4,128)S(1)} async-done(((f32[64,4,128]{2,1,0:T(4,128)}), f32[64,4,128]{2,1,0:T(4,128)S(1)}, u32[]{:S(2)}, u32[]{:S(2)}) %all-to-all-start.1) | async-done | bytes 131104 | tf_op jit(solution)/shard_map/statistics/all_to_all | solution.py:336
  74.9 2.3 %scale.1 = bf16[64,72,128]{2,1,0:T(8,128)(2,1)S(1)} custom-call(f32[256,128]{1,0:T(8,128)S(1)} %bitcast.20, f32[128,4096]{1,0:T(8,128)} %get-tuple-element.19.soft_in, bf16[128,4096]{1,0:T(8,128)(2,1)} %get-tuple-element.20.picked_in, f32[272,128]{1,0:T(8,128)S(1)} %get-tuple-element.21.columns), custom_call_target="tpu_custom_call" | custom-call | flops 2000000 | bytes 4194304 | tf_op jit(solution)/shard_map/scale/pallas_call | solution.py:75
  77.2 38.9 %all_to_all.15.blocks = bf16[64,72,128]{2,1,0:T(8,128)(2,1)S(1)} all-to-all(bf16[64,72,128]{2,1,0:T(8,128)(2,1)S(1)} %scale.1), channel_id=1, replica_groups={{0,2,4,6,8,10,12,14,16,18,20,22,24,26,28,30,32,34,36,38,40,42,44,46,48,..., dimensions={0} | all-to-all | bytes 2359296 | tf_op jit(solution)/shard_map/scatter_dnormed/all_to_all | solution.py:336
  116.1 0.4 features.1
  116.5 1.9 %collective-permute-start.5 = (f32[16,32]{1,0:T(8,128)S(1)}, f32[16,32]{1,0:T(8,128)S(1)}, u32[]{:S(2)}, u32[]{:S(2)}) collective-permute-start(f32[16,32]{1,0:T(8,128)S(1)} %get-tuple-element.30), channel_id=1, source_target_pairs={{0,1},{1,0},{2,3},{3,2},{4,5},{5,4},{6,7},{7,6},{8,9},{9,8},{10,11... | collective-permute-start | bytes 6152 | tf_op jit(solution)/shard_map/features/ppermute | solution.py:457
  118.4 1.0 resid_grad.1
  119.4 0.1 collective-permute-done.5
  119.6 0.6 fusion.3
  (19 shorter events, 0.1 us)
Async XLA Ops:
  0.6 18.5 %copy-start = (bf16[2,224,256]{2,1,0:T(8,128)(2,1)S(1)}, bf16[2,224,256]{2,1,0:T(8,128)(2,1)}, u32[]{:S(2)}) copy-start(bf16[2,224,256]{2,1,0:T(8,128)(2,1)} %gate_up.1) | copy-start | bytes 688132
  0.6 0.8 copy-start.1
  1.4 17.8 %copy-start.4 = (s32[224]{0:T(256)S(1)}, s32[224]{0:T(256)}, u32[]{:S(2)}) copy-start(s32[224]{0:T(256)} %param.16) | copy-start | bytes 2692
  1.4 18.2 %copy-start.6 = (s32[512]{0:T(512)S(1)}, s32[512]{0:T(512)}, u32[]{:S(2)}) copy-start(s32[512]{0:T(512)} %param.15) | copy-start | bytes 6148
  2.6 46.4 %all-to-all-start = ((bf16[64,64,128]{2,1,0:T(8,128)(2,1)}), bf16[64,64,128]{2,1,0:T(8,128)(2,1)S(1)}, u32[]{:S(2)}, u32[]{:S(2)}) async-start(bf16[64,64,128]{2,1,0:T(8,128)(2,1)} %gather_hidden.1), calls=%async_computation | async-start | bytes 2097152 | tf_op jit(solution)/shard_map/gather_hidden/all_to_all | solution.py:336
  19.7 15.2 %copy-start.7 = (s32[256]{0:T(256)S(1)}, s32[256]{0:T(256)}, u32[]{:S(2)}) copy-start(s32[256]{0:T(256)} %param.13) | copy-start | bytes 3076
  19.7 15.4 %copy-start.8 = (s32[256]{0:T(256)S(1)}, s32[256]{0:T(256)}, u32[]{:S(2)}) copy-start(s32[256]{0:T(256)} %param.14) | copy-start | bytes 3076
  19.7 15.9 %copy-start.5 = (bf16[4096]{0:T(1024)(128)(2,1)S(1)}, bf16[4096]{0:T(1024)(128)(2,1)}, u32[]{:S(2)}) copy-start(bf16[4096]{0:T(1024)(128)(2,1)} %param.10) | copy-start | bytes 24580
  19.8 15.9 %copy-start.2 = (bf16[2,4096]{1,0:T(2,128)(2,1)S(1)}, bf16[2,4096]{1,0:T(2,128)(2,1)}, u32[]{:S(2)}) copy-start(bf16[2,4096]{1,0:T(2,128)(2,1)} %rows.1) | copy-start | bytes 49156
  19.8 16.0 %copy-start.3 = (s32[2,4096]{1,0:T(2,128)S(1)}, s32[2,4096]{1,0:T(2,128)}, u32[]{:S(2)}) copy-start(s32[2,4096]{1,0:T(2,128)} %codes.1) | copy-start | bytes 98308
  19.8 16.4 %collective-permute-start = (f32[68,128]{1,0:T(8,128)S(1)}, f32[68,128]{1,0:T(8,128)S(1)}, u32[]{:S(2)}, u32[]{:S(2)}) collective-permute-start(f32[68,128]{1,0:T(8,128)S(1)} %pad_maximum_fusion), channel_id=1, source_target_pairs={{0,1},{1,0},{2,3},{3,2},{4,5},{5,4},{6,7},{7,6},{8,9},{9,8},{10,11... | collective-permute-start | bytes 104456 | tf_op jit(solution)/shard_map/activations/ppermute | solution.py:363
  26.2 10.1 %collective-permute-start.1 = (bf16[128,4096]{1,0:T(8,128)(2,1)}, bf16[128,4096]{1,0:T(8,128)(2,1)}, u32[]{:S(2)}, u32[]{:S(2)}) collective-permute-start(bf16[128,4096]{1,0:T(8,128)(2,1)} %get-tuple-element.34), channel_id=1, source_target_pairs={{0,1},{1,0},{2,3},{3,2},{4,5},{5,4},{6,7},{7,6},{8,9},{9,8},{10,11... | collective-permute-start | bytes 3145736 | tf_op jit(solution)/shard_map/partner_rows/ppermute | solution.py:351
  28.6 7.7 %collective-permute-start.2 = (bf16[128,4096]{1,0:T(8,128)(2,1)}, bf16[128,4096]{1,0:T(8,128)(2,1)}, u32[]{:S(2)}, u32[]{:S(2)}) collective-permute-start(bf16[128,4096]{1,0:T(8,128)(2,1)} %get-tuple-element.33), channel_id=1, source_target_pairs={{0,1},{1,0},{2,3},{3,2},{4,5},{5,4},{6,7},{7,6},{8,9},{9,8},{10,11... | collective-permute-start | bytes 3145736 | tf_op jit(solution)/shard_map/partner_rows/ppermute | solution.py:351
  30.5 5.8 %collective-permute-start.3 = (bf16[128,4096]{1,0:T(8,128)(2,1)}, bf16[128,4096]{1,0:T(8,128)(2,1)}, u32[]{:S(2)}, u32[]{:S(2)}) collective-permute-start(bf16[128,4096]{1,0:T(8,128)(2,1)} %get-tuple-element.32), channel_id=1, source_target_pairs={{0,1},{1,0},{2,3},{3,2},{4,5},{5,4},{6,7},{7,6},{8,9},{9,8},{10,11... | collective-permute-start | bytes 3145736 | tf_op jit(solution)/shard_map/partner_rows/ppermute | solution.py:351
  32.9 4.9 %collective-permute-start.4 = (bf16[128,4096]{1,0:T(8,128)(2,1)}, bf16[128,4096]{1,0:T(8,128)(2,1)}, u32[]{:S(2)}, u32[]{:S(2)}) collective-permute-start(bf16[128,4096]{1,0:T(8,128)(2,1)} %get-tuple-element.31), channel_id=1, source_target_pairs={{0,1},{1,0},{2,3},{3,2},{4,5},{5,4},{6,7},{7,6},{8,9},{9,8},{10,11... | collective-permute-start | bytes 3145736 | tf_op jit(solution)/shard_map/partner_rows/ppermute | solution.py:351
  55.7 19.2 %all-to-all-start.1 = ((f32[64,4,128]{2,1,0:T(4,128)}), f32[64,4,128]{2,1,0:T(4,128)S(1)}, u32[]{:S(2)}, u32[]{:S(2)}) async-start(f32[64,4,128]{2,1,0:T(4,128)} %bitcast.7), calls=%async_computation.1 | async-start | bytes 262144 | tf_op jit(solution)/shard_map/statistics/all_to_all | solution.py:336
  116.5 3.1 %collective-permute-start.5 = (f32[16,32]{1,0:T(8,128)S(1)}, f32[16,32]{1,0:T(8,128)S(1)}, u32[]{:S(2)}, u32[]{:S(2)}) collective-permute-start(f32[16,32]{1,0:T(8,128)S(1)} %get-tuple-element.30), channel_id=1, source_target_pairs={{0,1},{1,0},{2,3},{3,2},{4,5},{5,4},{6,7},{7,6},{8,9},{9,8},{10,11... | collective-permute-start | bytes 6152 | tf_op jit(solution)/shard_map/features/ppermute | solution.py:457
